TPU v7x, 512 devices: a whole 4x8x8 slice. The times are simulated.
512 devices in a mesh: mem: 8 (over x, core), sp: 64 (over z, y).
Axes of the slice: x: 4, y: 8, z: 8, core: 2. Of those that a mesh axis runs over, the one named last changes fastest.
Arguments:
- control: float32 [16, 256, 512], P('mem', 'sp'), may hold values from -6 to 6
- gradient: float32 [16, 256, 512], P('mem', 'sp'), may hold values from -6 to 6
- direction: float32 [16, 256, 512], P('mem', 'sp'), may hold values from -6 to 6
- perturb: bfloat16 [16, 2, 3072, 1536], P('mem', None, 'sp'), may hold values from -6 to 6
- obs_index: int32 [64, 2048], P('sp'), may hold values from 0 to 147455
- obs_count: int32 [64], P('sp'), may hold values from 1024 to 2048, as said below
- obs_weight: float32 [64, 2048], P('sp'), may hold values from 50 to 800
- cutoff: int32 [1], replicated, may hold values from 24 to 64
Outputs:
- control_new: float32 [16, 256, 512], P('mem', 'sp')
- gradient_new: float32 [16, 256, 512], P('mem', 'sp')
- direction_new: float32 [16, 256, 512], P('mem', 'sp')
Inputs may be any that keep to these rules, and one draw needn't show every extreme that they name: `obs_count`: at least one pencil uses all 2048 slots; every pencil uses at least half of them.
All inputs are finite; a program needn't handle non-finite values.
Results may differ from a plain program's by a relative error of at most 0.00035.
Values sent between devices are 32-bit elements; how exact they have to be, the bound alone decides.
No kernel may reach another device: no remote copies, remote signals or barrier semaphores. Data moves between devices by JAX's collectives and lax.ppermute only.
A program may use at most 64 MiB of HBM per device.

v0:
```python
import math

import jax
import jax.numpy as jnp
from jax import lax
from jax.sharding import PartitionSpec as P

highest_mode = lax.Precision.HIGHEST


def wave_number(modes):
    column = jnp.arange(2 * modes, dtype=jnp.int32)
    return jnp.where(column < modes, column, column - modes + 1)


def basis_table(points, modes, length):
    grid_row = jnp.arange(points, dtype=jnp.int32)[:, None]
    column = jnp.arange(2 * modes, dtype=jnp.int32)[None, :]
    wavenum = jnp.where(column < modes, column, column - modes + 1)
    residue = wavenum * grid_row % length
    phase_angle = 2.0 * math.pi / length * residue.astype(jnp.float32)
    return jnp.where(column < modes, jnp.cos(phase_angle), jnp.sin(phase_angle))


def amplitude(cutoff, modes_a, modes_b):
    wave_a = wave_number(modes_a)[None, :]
    wave_b = wave_number(modes_b)[:, None]
    radius = wave_a * wave_a + 4 * wave_b * wave_b
    retained = 4096 * radius <= cutoff[0] * cutoff[0] * modes_a * modes_a
    shape_factor = 1.0 / (1.0 + 16.0 / (modes_a * modes_a) * radius.astype(jnp.float32))
    masked = jnp.where(retained, shape_factor, jnp.zeros_like(shape_factor))
    energy = jnp.sum(masked * masked)
    return masked * jnp.sqrt(2.0 / energy)


def shards(control, gradient, direction, perturb, obs_index, obs_count, obs_weight, cutoff):
    mem_local, level_count, row_count, points_b = perturb.shape
    spread = lax.axis_size("sp")
    local_modes_b = direction.shape[1]
    modes_a = direction.shape[2] // 2
    modes_b = local_modes_b * spread // 2
    points_a = row_count * spread
    members_all = mem_local * lax.axis_size("mem")
    member_scale = 1.0 / math.sqrt(members_all - 1)
    pencil = lax.axis_index("sp")
    amp_full = amplitude(cutoff, modes_a, modes_b)
    amp_local = lax.dynamic_slice_in_dim(amp_full, pencil * local_modes_b, local_modes_b, 0)
    table_a = basis_table(points_a, modes_a, points_a)
    second_table = basis_table(points_b, modes_b, points_b)
    spectral = amp_local[None] * direction
    partial_a = jnp.einsum("mka,na->mkn", spectral, table_a, precision=highest_mode)
    grid_field = jnp.einsum(
        "dul,ou->dlo",
        lax.all_to_all(partial_a, "sp", split_axis=2, concat_axis=1, tiled=True),
        second_table,
        precision=highest_mode,
    )
    partial_value = (
        jnp.einsum(
            "aegd,agd->egd",
            perturb,
            grid_field,
            precision=highest_mode,
            preferred_element_type=jnp.float32,
        )
        * member_scale
    )
    flat_index = obs_index[0]
    increment = lax.psum(partial_value, "mem")
    sampled = increment.reshape(-1)[flat_index]
    usable = jnp.arange(flat_index.shape[0], dtype=jnp.int32) < obs_count[0]
    weighted = jnp.where(usable, obs_weight[0] * sampled, jnp.zeros_like(sampled))
    adjoint_field = (
        jnp.zeros((level_count * row_count * points_b,), jnp.float32).at[flat_index].add(weighted)
    )
    adjoint_field = adjoint_field.reshape(level_count, row_count, points_b)
    reduced_total = (
        jnp.einsum(
            "hnvy,nvy->hvy",
            perturb,
            adjoint_field,
            precision=highest_mode,
            preferred_element_type=jnp.float32,
        )
        * member_scale
    )
    partial_sum_second = jnp.einsum(
        "nou,ui->nio", reduced_total, second_table, precision=highest_mode
    )
    back_spectra = jnp.einsum(
        "mkn,na->mka",
        lax.all_to_all(partial_sum_second, "sp", split_axis=1, concat_axis=2, tiled=True),
        table_a,
        precision=highest_mode,
    )
    product = direction + amp_local[None] * back_spectra
    grad_sq = lax.psum(jnp.sum(gradient * gradient), ("mem", "sp"))
    curvature = lax.psum(jnp.sum(direction * product), ("mem", "sp"))
    step_length = grad_sq / curvature
    gradient_new = gradient + step_length * product
    new_sq = lax.psum(jnp.sum(gradient_new * gradient_new), ("mem", "sp"))
    control_new = control + step_length * direction
    direction_new = -gradient_new + new_sq / grad_sq * direction
    return (control_new, gradient_new, direction_new)


def solution(mesh):
    placed = (
        P("mem", "sp", None),
        P("mem", "sp", None),
        P("mem", "sp", None),
        P("mem", None, "sp", None),
        P("sp", None),
        P("sp"),
        P("sp", None),
        P(),
    )
    return jax.shard_map(
        shards,
        mesh=mesh,
        in_specs=placed,
        out_specs=(P("mem", "sp", None), P("mem", "sp", None), P("mem", "sp", None)),
        check_vma=False,
    )
```

profile of v0, /device:TPU:1, one launch (start us, length us, event | category | flops | bytes accessed | tf_op | source)
XLA Modules:
  0.0 463.0 jit_solution(5490580796986929539)
XLA Ops:
  7.9 0.9 multiply_reduce_fusion.2
  9.5 32.0 %fusion.4 = f32[2,4,3072]{2,1,0:T(4,128)S(1)} fusion(s32[512]{0:T(512)S(1)} %iota_select_fusion, pred[512]{0:T(512)(128)(4,1)S(1)} %iota_compare_fusion.1, f32[2,4,512]{2,1,0:T(4,128)} %param.10, f32[4,512]{1,0:T(4,128)S(1)} %dynamic-slice_multiply_fusion), kind=kOutput, calls=%fused_computation.7 | convolution fusion | flops 166727680 | bytes 125440 | tf_op jit(solution)/shard_map/mka,na->mkn/dot_general | solution.py:51
  41.5 2.9 copy.15
  44.5 5.6 %reshape.116 = f32[64,1,384]{2,1,0:T(1,128)} reshape(f32[3072,2,4]{2,1,0:T(2,128)S(1)} %bitcast.64) | data formatting | bytes 196608
  50.0 17.1 %all-to-all-start = ((f32[64,1,384]{2,1,0:T(1,128)}), f32[64,1,384]{2,1,0:T(1,128)S(1)}, u32[]{:S(2)}, u32[]{:S(2)}) async-start(f32[64,1,384]{2,1,0:T(1,128)} %reshape.116), calls=%async_computation | async-start | bytes 196608 | tf_op jit(solution)/shard_map/all_to_all | solution.py:54
  67.2 0.5 all-reduce.3.cloned.1.call-start
  67.7 10.9 %all-to-all-done = f32[64,1,384]{2,1,0:T(1,128)S(1)} async-done(((f32[64,1,384]{2,1,0:T(1,128)}), f32[64,1,384]{2,1,0:T(1,128)S(1)}, u32[]{:S(2)}, u32[]{:S(2)}) %all-to-all-start) | async-done | bytes 98336 | tf_op jit(solution)/shard_map/all_to_all | solution.py:54
  78.6 0.5 broadcast.132
  79.1 0.9 reduce.4
  80.0 4.8 %reshape.117 = f32[3072,2,4]{2,1,0:T(2,128)S(1)} reshape(f32[64,384]{1,0:T(8,128)S(1)} %reduce.4) | data formatting | bytes 196608
  84.8 1.7 copy.37
  86.5 0.2 copy.17
  86.7 0.0 copy-start
  86.7 8.7 %convolution_bitcast_fusion = f32[48,1536,2]{1,0,2:T(8,128)S(1)} fusion(f32[2,256,48]{2,1,0:T(8,128)S(1)} %bitcast.71, s32[256]{0:T(256)S(1)} %iota_select_fusion.1, pred[256]{0:T(512)(128)(4,1)S(1)} %iota_compare_fusion.2), kind=kOutput, calls=%fused_computation.24 | convolution fusion | flops 456916992 | bytes 689408 | tf_op jit(solution)/shard_map/dul,ou->dlo/dot_general | solution.py:52
  95.4 0.0 copy-done
  95.4 0.1 multiply_reduce_fusion.1
  95.6 0.0 copy-start.6
  95.6 0.1 multiply_bitcast_fusion
  95.6 0.8 reshape.90
  96.5 0.0 all-reduce.3.cloned.1.call-update
  96.5 0.0 copy-done.6
  97.2 0.0 copy-start.5
  97.2 62.6 %all-reduce.3.cloned.1.call-done = f32[147456]{0:T(1024)} async-done(((f32[147456]{0:T(1024)}), f32[147456]{0:T(1024)}) %all-reduce.3.cloned.1.call-update) | async-done | bytes 589840 | tf_op jit(solution)/shard_map/psum | solution.py:69
  159.8 24.5 %gather_fusion = f32[2048]{0:T(1024)S(1)} fusion(f32[147456]{0:T(1024)} %all-reduce.3.cloned.1.call-done, s32[2048]{0:T(1024)S(1)} %broadcast_clamp_fusion), kind=kCustom, calls=%fused_computation | custom fusion | bytes 24576 | tf_op jit(solution)/shard_map/gather | solution.py:70
  184.3 0.0 copy-done.5
  184.3 11.6 %scatter_custom_fusion = f32[147456]{0:T(1024)S(1)} fusion(s32[2048]{0:T(1024)S(1)} %bitcast.74, f32[2048]{0:T(1024)S(1)} %multiply_select_fusion, f32[]{:T(128)} %constant.22.clone.1), kind=kCustom, calls=%fused_computation.63 | custom fusion | flops 2048 | bytes 589828 | tf_op jit(solution)/shard_map/scatter-add | solution.py:74
  195.9 0.1 reshape.91
  196.0 0.1 multiply_reduce_fusion
  196.1 0.0 copy-start.1
  196.1 7.5 %fusion.27 = f32[2,256,48]{1,2,0:T(8,128)S(1)} fusion(s32[256]{0:T(256)S(1)} %iota_select_fusion.1, pred[256]{0:T(512)(128)(4,1)S(1)} %iota_compare_fusion.2, f32[48,1536,2]{1,0,2:T(8,128)S(1)} %multiply_reduce_fusion), kind=kOutput, calls=%fused_computation.38 | convolution fusion | flops 457064448 | bytes 689408 | tf_op jit(solution)/shard_map/nou,ui->nio/dot_general | solution.py:87
  203.6 0.0 copy-start.3
  203.6 0.1 copy.19
  203.8 1.1 reshape.118
  204.8 12.7 %all-to-all-start.1 = ((f32[64,1,384]{2,1,0:T(1,128)}), f32[64,1,384]{2,1,0:T(1,128)S(1)}, u32[]{:S(2)}, u32[]{:S(2)}) async-start(f32[64,1,384]{2,1,0:T(1,128)} %reshape.118), calls=%async_computation.1 | async-start | bytes 196608 | tf_op jit(solution)/shard_map/all_to_all | solution.py:92
  217.5 0.0 copy-done.1
  217.5 0.6 multiply_reduce_fusion.5
  218.1 10.7 %all-to-all-done.1 = f32[64,1,384]{2,1,0:T(1,128)S(1)} async-done(((f32[64,1,384]{2,1,0:T(1,128)}), f32[64,1,384]{2,1,0:T(1,128)S(1)}, u32[]{:S(2)}, u32[]{:S(2)}) %all-to-all-start.1) | async-done | bytes 98336 | tf_op jit(solution)/shard_map/all_to_all | solution.py:92
  228.8 0.9 reduce.5
  229.7 0.4 reshape.119
  230.2 0.2 all_to_all.33
  230.4 0.0 copy-done.3
  230.4 0.0 copy-start.4
  230.4 30.2 %multiply_reduce_fusion.4 = (f32[]{:T(128)}, f32[2,4,512]{2,1,0:T(4,128)S(1)}) fusion(f32[2,4,512]{2,1,0:T(4,128)S(1)} %copy-done.3, f32[2,4,3072]{2,1,0:T(4,128)S(1)} %all_to_all.33, s32[512]{0:T(512)S(1)} %iota_select_fusion, pred[512]{0:T(512)(128)(4,1)S(1)} %iota_compare_fusion.1, f32[4,512]{1,0:T(4,128)S(1)} %dynamic-slice_multiply_fusion), kind=kOutput, calls=%fused_computation.70 | convolution fusion | flops 166739968 | bytes 141828 | tf_op jit(solution)/shard_map/mkn,na->mka/dot_general | solution.py:90
  260.6 96.3 %all-reduce = (f32[]{:T(128)}, f32[]{:T(128)}) all-reduce(f32[]{:T(128)} %multiply_reduce_fusion.5, f32[]{:T(128)} %get-tuple-element.11), channel_id=1, replica_groups=mesh['mem'=8,'sp'=64] {'mem','sp'}, use_global_device_ids=true, to_apply=%region_1.2 | all-reduce | flops 2 | bytes 16 | tf_op jit(solution)/shard_map/psum | solution.py:97
  358.2 0.6 multiply_reduce_fusion.3
  358.8 95.2 %psum.31 = f32[]{:T(128)} all-reduce(f32[]{:T(128)} %get-tuple-element.5), channel_id=1, replica_groups=mesh['mem'=8,'sp'=64] {'mem','sp'}, use_global_device_ids=true, to_apply=%region_8.9 | all-reduce | flops 1 | bytes 8 | tf_op jit(solution)/shard_map/psum | solution.py:101
  455.3 0.0 copy-done.4
  455.3 0.6 multiply_add_fusion
  (14 shorter events, 0.1 us)
Async XLA Ops:
  50.0 28.5 %all-to-all-start = ((f32[64,1,384]{2,1,0:T(1,128)}), f32[64,1,384]{2,1,0:T(1,128)S(1)}, u32[]{:S(2)}, u32[]{:S(2)}) async-start(f32[64,1,384]{2,1,0:T(1,128)} %reshape.116), calls=%async_computation | async-start | bytes 196608 | tf_op jit(solution)/shard_map/all_to_all | solution.py:54
  67.2 92.6 %all-reduce.3.cloned.1.call-start = ((), (), s32[]{:S(2)}) async-start(), calls=%async_computation.2 | async-start | bytes 1179648 | tf_op jit(solution)/shard_map/psum | solution.py:69
  86.7 8.7 %copy-start = (bf16[2,2,48,1536]{3,2,1,0:T(8,128)(2,1)S(1)}, bf16[2,2,48,1536]{3,2,1,0:T(8,128)(2,1)}, u32[]{:S(2)}) copy-start(bf16[2,2,48,1536]{3,2,1,0:T(8,128)(2,1)} %param.11) | copy-start | bytes 1769476
  95.6 0.9 copy-start.6
  97.2 87.1 %copy-start.5 = (f32[1,2048]{1,0:T(1,128)S(1)}, f32[1,2048]{1,0:T(1,128)}, u32[]{:S(2)}) copy-start(f32[1,2048]{1,0:T(1,128)} %param.14) | copy-start | bytes 24580
  196.1 21.4 %copy-start.1 = (f32[2,4,512]{2,1,0:T(4,128)S(1)}, f32[2,4,512]{2,1,0:T(4,128)}, u32[]{:S(2)}) copy-start(f32[2,4,512]{2,1,0:T(4,128)} %param.9) | copy-start | bytes 49156
  203.6 26.8 %copy-start.3 = (f32[2,4,512]{2,1,0:T(4,128)S(1)}, f32[2,4,512]{2,1,0:T(4,128)}, u32[]{:S(2)}) copy-start(f32[2,4,512]{2,1,0:T(4,128)} %param.10) | copy-start | bytes 49156
  204.8 24.0 %all-to-all-start.1 = ((f32[64,1,384]{2,1,0:T(1,128)}), f32[64,1,384]{2,1,0:T(1,128)S(1)}, u32[]{:S(2)}, u32[]{:S(2)}) async-start(f32[64,1,384]{2,1,0:T(1,128)} %reshape.118), calls=%async_computation.1 | async-start | bytes 196608 | tf_op jit(solution)/shard_map/all_to_all | solution.py:92
  230.4 224.9 %copy-start.4 = (f32[2,4,512]{2,1,0:T(4,128)S(1)}, f32[2,4,512]{2,1,0:T(4,128)}, u32[]{:S(2)}) copy-start(f32[2,4,512]{2,1,0:T(4,128)} %param.8) | copy-start | bytes 49156
  358.8 97.2 %copy-start.2 = (f32[2,4,512]{2,1,0:T(4,128)}, f32[2,4,512]{2,1,0:T(4,128)S(1)}, u32[]{:S(2)}) copy-start(f32[2,4,512]{2,1,0:T(4,128)S(1)} %get-tuple-element.6) | copy-start | bytes 49156
Sparse Core Ops, SparseCore 0:
  96.6 63.1 all-reduce.2
where the time goes:
time: 472 us; the launch traced here: 463 us
  blocking collectives  191 us (40%)
  waiting for transfers between devices  84.1 us (18%)
  matrix products  78.3 us (17%)
  local copies, waits for them, and re-layouts  43.1 us (9%)
  starting transfers between devices  30.3 us (6%)
  between operations  19.3 us (4%)
  other arithmetic  16.4 us (3%)
    psum x1, blocking collectives, shards(): grad_sq = lax.psum(jnp.sum(gradient * gradient), ('mem', 'sp'))  96.3 us
    psum x1, blocking collectives, shards(): new_sq = lax.psum(jnp.sum(gradient_new * gradient_new), ('mem', 'sp'))  95.2 us
    psum x1, waiting for transfers between devices, shards(): increment = lax.psum(partial_value, 'mem')  62.6 us
    dot_general x1, matrix products, shards(): jnp.einsum('mka,na->mkn', spectral, table_a, precision=highest_mode)  32 us
    dot_general x1, matrix products, shards(): jnp.einsum('mkn,na->mka', lax.all_to_all(partial_sum_second, 'sp', split_...  30.2 us
    gather x1, local copies, waits for them, and re-layouts, shards(): sampled = increment.reshape(-1)[flat_index]  24.5 us
    all_to_all x1, starting transfers between devices, shards(): lax.all_to_all(partial_a, 'sp', split_axis=2, concat_axis=1, tiled=True)  17.1 us
    all_to_all x1, starting transfers between devices, shards(): lax.all_to_all(partial_sum_second, 'sp', split_axis=1, concat_axis=2, til...  12.7 us
  transfers between devices with their start and end apart: 3, of which 3 were waited for; matrix products, arithmetic and copies ran while one was open for 0% of the time, Pallas kernels for 0%

commit v1 on v0

v1 whole, which is shorter than its diff:
```python
import functools
import math

import jax
import jax.numpy as jnp
import numpy as np
from jax import lax
from jax.experimental import pallas as pl
from jax.experimental.pallas import tpu as pltpu
from jax.sharding import PartitionSpec as P

NA, NB, KA, KB = 3072, 1536, 256, 128
LEVELS, SLOTS, MEMBERS, ROWS, N_SP = 2, 2048, 16, 48, 64
LOCAL_M, LOCAL_KB = 2, 4
SIDE = 8
SCALE = 1.0 / math.sqrt(MEMBERS - 1)
CHUNK = LOCAL_KB * LOCAL_M * ROWS

f32, bf16, i32 = jnp.float32, jnp.bfloat16, jnp.int32
VMEM = pl.BlockSpec(memory_space=pltpu.VMEM)
HBM = pl.BlockSpec(memory_space=pltpu.HBM)
SMEM = pl.BlockSpec(memory_space=pltpu.SMEM)
PARAMS = pltpu.CompilerParams(vmem_limit_bytes=40 * 1024 * 1024)
WHOLE = pltpu.CompilerParams(vmem_limit_bytes=60 * 1024 * 1024)


def tables():
    w = np.arange(KA, dtype=np.int64)
    s = np.arange(N_SP, dtype=np.int64)[:, None]
    turn = 2.0 * np.pi * ((s * w) % N_SP) / N_SP
    r = np.arange(ROWS, dtype=np.int64)[:, None]
    ws = np.where(w == 0, KA, w)
    cos_rows = np.cos(2.0 * np.pi * ((r * w) % NA) / NA)
    sin_rows = np.sin(2.0 * np.pi * ((r * ws) % NA) / NA)
    rows = np.concatenate([cos_rows, sin_rows], axis=1).astype(np.float32)
    high = rows.astype(jnp.bfloat16)
    low = (rows - high.astype(np.float32)).astype(jnp.bfloat16)
    phase = np.stack([np.cos(turn), np.sin(turn)]).astype(np.float32)
    return phase, np.stack([high, low])


def split(x):
    high = x.astype(bf16)
    return high, (x - high.astype(f32)).astype(bf16)


def dot(a, b, dims):
    return lax.dot_general(a, b, (dims, ((), ())), preferred_element_type=f32)


def wave(column, modes):
    return jnp.where(column < modes, column, column - modes + 1)


def shape_factor(radius, cutoff):
    retained = 4096 * radius <= cutoff * cutoff * (KA * KA)
    factor = 1.0 / (1.0 + (16.0 / (KA * KA)) * radius.astype(f32))
    return jnp.where(retained, factor, 0.0)


def to_rows(cut_ref, pen_ref, dir_in, phase_in, rows_in, out_ref, amp_ref, high_ref, low_ref, dir_ref, phase_ref,
            rows_ref, sems):
    pairs = ((dir_in, dir_ref), (phase_in, phase_ref), (rows_in, rows_ref))
    copies = [pltpu.make_async_copy(a, b, sems.at[i]) for i, (a, b) in enumerate(pairs)]
    for copy in copies:
        copy.start()
    cutoff, pencil = cut_ref[0], pen_ref[0]
    wa = lax.broadcasted_iota(i32, (1, 384), 1)
    wb = lax.broadcasted_iota(i32, (136, 1), 0)
    count_a = jnp.where(wa > KA, 0.0, jnp.where((wa == 0) | (wa == KA), 1.0, 2.0))
    count_b = jnp.where(wb > KB, 0.0, jnp.where((wb == 0) | (wb == KB), 1.0, 2.0))
    factor = shape_factor(wa * wa + 4 * (wb * wb), cutoff)
    energy = jnp.sum(factor * factor * count_a * count_b, axis=0, keepdims=True)
    energy = jnp.sum(energy, axis=1, keepdims=True)
    gain = jnp.sqrt(2.0 / energy)
    wa = wave(lax.broadcasted_iota(i32, (1, 2 * KA), 1), KA)
    wb = wave(lax.broadcasted_iota(i32, (LOCAL_KB, 1), 0) + pencil * LOCAL_KB, KB)
    amp = shape_factor(wa * wa + 4 * (wb * wb), cutoff) * gain
    amp_ref[...] = amp

    for copy in copies:
        copy.wait()
    phase_c, phase_s = phase_ref[0], phase_ref[1]
    for m in range(LOCAL_M):
        spectral = amp * dir_ref[m]
        part_c = spectral[:, :KA]
        part_s = pltpu.roll(spectral[:, KA:], 1, 1)
        for k in range(LOCAL_KB):
            c, s = part_c[k:k + 1], part_s[k:k + 1]
            at = pl.ds((k * LOCAL_M + m) * N_SP, N_SP)
            for half, value in ((0, c * phase_c + s * phase_s), (1, s * phase_c - c * phase_s)):
                high, low = split(value)
                high_ref[at, half * KA:(half + 1) * KA] = high
                low_ref[at, half * KA:(half + 1) * KA] = low
    nt = ((1,), (1,))
    result = (dot(high_ref[...], rows_ref[0], nt) + dot(high_ref[...], rows_ref[1], nt)
              + dot(low_ref[...], rows_ref[0], nt))
    for i in range(LOCAL_M * LOCAL_KB):
        out_ref[:, 0, i * ROWS:(i + 1) * ROWS] = result[i * N_SP:(i + 1) * N_SP]


def cell_parts(index_ref):
    index = index_ref[...]
    line = jnp.floor((index.astype(f32) + 0.5) * (1.0 / NB)).astype(i32)
    column = index - line * NB
    return line, column


def turns_to_cos_sin(turns):
    quarter = jnp.floor(turns * 4.0 + 0.5)
    x = (turns - quarter * 0.25) * (2.0 * math.pi)
    x2 = x * x
    s = x * (1.0 + x2 * (-1.0 / 6 + x2 * (1.0 / 120 + x2 * (-1.0 / 5040 + x2 * (1.0 / 362880)))))
    c = 1.0 + x2 * (-0.5 + x2 * (1.0 / 24 + x2 * (-1.0 / 720 + x2 * (1.0 / 40320))))
    q = quarter.astype(i32) & 3
    odd = (q & 1) == 1
    cos = jnp.where(odd, s, c)
    sin = jnp.where(odd, c, s)
    return jnp.where((q == 1) | (q == 2), -cos, cos), jnp.where(q >= 2, -sin, sin)


def residue_turns(wavenum, column):
    product = wavenum * column
    return (product - jnp.floor(product * (1.0 / NB)) * NB) * (1.0 / NB)


def at_slots(index_ref, pert_ref, basis_ref, values_ref):
    block = 256

    @pl.loop(0, SLOTS // block)
    def _(step):
        at = pl.ds(pl.multiple_of(step * block, block), block)
        index = index_ref[:, at]
        line = jnp.floor((index.astype(f32) + 0.5) * (1.0 / NB)).astype(i32)
        column = index - line * NB
        place = column.astype(f32)
        y = lax.broadcasted_iota(i32, (SIDE, 1), 0)
        cos_y, sin_y = turns_to_cos_sin(residue_turns((4 * y).astype(f32), place))
        q = lax.broadcasted_iota(i32, (SIDE * LOCAL_KB, 1), 0)
        is_sin = (q & 7) >= SIDE // 2
        wq = (32 * (q & 3) + (q >> 3) + is_sin.astype(i32)).astype(f32)
        cos_q, sin_q = turns_to_cos_sin(residue_turns(wq, place) - jnp.where(is_sin, 0.25, 0.0))
        for pair in range(SIDE * LOCAL_KB // 2):
            both = [cos_y * cos_q[g:g + 1] - sin_y * sin_q[g:g + 1] for g in (2 * pair, 2 * pair + 1)]
            high, low = split(jnp.concatenate(both, axis=0))
            basis_ref[0, pair * 16:(pair + 1) * 16, at] = high
            basis_ref[1, pair * 16:(pair + 1) * 16, at] = low
        lines = LEVELS * ROWS
        grid_column = lax.broadcasted_iota(i32, (NB, block), 0)
        chosen = jnp.where(grid_column == column, 1.0, 0.0).astype(bf16)
        found = dot(pert_ref[...], chosen, ((1,), (0,)))
        mine = lax.broadcasted_iota(i32, (lines, block), 0) == line
        for m in range(LOCAL_M):
            part = jnp.where(mine, found[m * lines:(m + 1) * lines], 0.0)
            values_ref[m:m + 1, at] = jnp.sum(part, axis=0, keepdims=True)


def sample(recv_ref, basis_ref, values_ref, index_ref, out_ref):
    wide = LOCAL_M * ROWS
    field = jnp.concatenate([recv_ref[:, 0, k * wide:(k + 1) * wide] for k in range(LOCAL_KB)], axis=0)
    high, low = split(field.T)
    nn = ((1,), (0,))
    both = dot(jnp.concatenate([high, low], axis=0), basis_ref[0], nn)
    rows = both[:wide] + both[wide:] + dot(high, basis_ref[1], nn)
    line, _ = cell_parts(index_ref)
    row = jnp.where(line >= ROWS, line - ROWS, line)
    mine = lax.broadcasted_iota(i32, (ROWS, SLOTS), 0) == row
    total = jnp.zeros((1, SLOTS), f32)
    for m in range(LOCAL_M):
        part = jnp.sum(jnp.where(mine, rows[m * ROWS:(m + 1) * ROWS], 0.0), axis=0, keepdims=True)
        total += values_ref[m:m + 1] * part
    out_ref[...] = total * SCALE


def spread(count_ref, parts_ref, weight_ref, basis_ref, values_ref, index_ref, out_ref):
    sampled = jnp.sum(parts_ref[...], axis=0)
    usable = lax.broadcasted_iota(i32, (1, SLOTS), 1) < count_ref[0]
    weighted = jnp.where(usable, weight_ref[...] * sampled, 0.0) * SCALE
    line, _ = cell_parts(index_ref)
    row = jnp.where(line >= ROWS, line - ROWS, line)
    mine = lax.broadcasted_iota(i32, (ROWS, SLOTS), 0) == row
    highs, lows = [], []
    for m in range(LOCAL_M):
        value = values_ref[m:m + 1] * weighted
        high = value.astype(bf16).astype(f32)
        highs.append(jnp.where(mine, high, 0.0).astype(bf16))
        lows.append(jnp.where(mine, value - high, 0.0).astype(bf16))
    empty = jnp.zeros((32, SLOTS), bf16)
    right = jnp.concatenate(highs + [empty] + lows + [empty], axis=0)
    nt = ((1,), (1,))
    both = dot(basis_ref[0], right, nt)
    result = both[:, :128] + both[:, 128:] + dot(basis_ref[1], right[:128], nt)
    wide = LOCAL_M * ROWS
    for k in range(LOCAL_KB):
        out_ref[:, 0, k * wide:(k + 1) * wide] = result[k * N_SP:(k + 1) * N_SP, :wide]


def fold(x):
    x = jnp.sum(x, axis=0, keepdims=True)
    return x[:, :128] + x[:, 128:256] + x[:, 256:384] + x[:, 384:]


def from_rows(recv_ref, phase_ref, rows_ref, amp_ref, dir_ref, grad_ref, prod_ref, sums_ref):
    count = LOCAL_M * LOCAL_KB
    left = jnp.concatenate([recv_ref[:, 0, i * ROWS:(i + 1) * ROWS] for i in range(count)], axis=0)
    high, low = split(left)
    nn = ((1,), (0,))
    turned = dot(high, rows_ref[0], nn) + dot(high, rows_ref[1], nn) + dot(low, rows_ref[0], nn)
    phase_c, phase_s = phase_ref[0], phase_ref[1]
    amp = amp_ref[...]
    totals = [jnp.zeros((1, 128), f32)] * 4
    for m in range(LOCAL_M):
        part_c, part_s = [], []
        for k in range(LOCAL_KB):
            i = k * LOCAL_M + m
            p, q = turned[i * N_SP:(i + 1) * N_SP, :KA], turned[i * N_SP:(i + 1) * N_SP, KA:]
            part_c.append(jnp.sum(p * phase_c - q * phase_s, axis=0, keepdims=True))
            part_s.append(jnp.sum(p * phase_s + q * phase_c, axis=0, keepdims=True))
        back_c = jnp.concatenate(part_c, axis=0)
        back_s = pltpu.roll(jnp.concatenate(part_s, axis=0), KA - 1, 1)
        d, g = dir_ref[m], grad_ref[m]
        product = d + amp * jnp.concatenate([back_c, back_s], axis=1)
        prod_ref[m] = product
        terms = (g * g, d * product, g * product, product * product)
        totals = [t + fold(x) for t, x in zip(totals, terms)]
    sums = jnp.concatenate(totals + [jnp.zeros((4, 128), f32)], axis=0)
    sums_ref[...] = sums


def update(parts_ref, cont_ref, grad_ref, dir_ref, prod_ref, cont_out, grad_out, dir_out):
    sums = jnp.sum(jnp.sum(parts_ref[...], axis=0), axis=1, keepdims=True)
    grad_sq, curvature, cross, prod_sq = [sums[i:i + 1] for i in range(4)]
    step = grad_sq / curvature
    new_sq = grad_sq + step * (2.0 * cross + step * prod_sq)
    ratio = new_sq / grad_sq
    for m in range(LOCAL_M):
        d = dir_ref[m]
        fresh = grad_ref[m] + step * prod_ref[m]
        cont_out[m] = cont_ref[m] + step * d
        grad_out[m] = fresh
        dir_out[m] = ratio * d - fresh


def call(kernel, in_specs, outs, scratch=(), flops=0, moved=0, params=PARAMS):
    shapes = [jax.ShapeDtypeStruct(shape, dtype) for shape, dtype in outs]
    return pl.pallas_call(
        kernel,
        out_shape=shapes,
        in_specs=in_specs,
        out_specs=[VMEM] * len(shapes),
        scratch_shapes=list(scratch),
        compiler_params=params,
        cost_estimate=pl.CostEstimate(flops=flops, bytes_accessed=moved, transcendentals=0),
    )


def stage_to_rows(cutoff, pencil, direction, phase, rows):
    return call(
        to_rows, [SMEM, SMEM, HBM, HBM, HBM],
        [((N_SP, 1, CHUNK), f32), ((LOCAL_KB, 2 * KA), f32)],
        [pltpu.VMEM((8 * N_SP, 2 * KA), bf16), pltpu.VMEM((8 * N_SP, 2 * KA), bf16),
         pltpu.VMEM((LOCAL_M, LOCAL_KB, 2 * KA), f32), pltpu.VMEM((2, N_SP, KA), f32),
         pltpu.VMEM((2, ROWS, 2 * KA), bf16), pltpu.SemaphoreType.DMA((3,))],
        flops=10 ** 8, moved=10 ** 6, params=WHOLE,
    )(cutoff, pencil, direction, phase, rows)


def stage_at_slots(index, perturb):
    return call(
        at_slots, [VMEM, VMEM],
        [((2, 2 * KB, SLOTS), bf16), ((LOCAL_M, SLOTS), f32)],
        flops=2 * 10 ** 9, moved=4 * 10 ** 6,
    )(index, perturb)


def stage_sample(recv, basis, values, index):
    return call(
        sample, [VMEM] * 4, [((1, SLOTS), f32)], flops=3 * 10 ** 8, moved=2 * 10 ** 6,
    )(recv, basis, values, index)[0]


def stage_spread(count, parts, weight, basis, values, index):
    return call(
        spread, [SMEM] + [VMEM] * 5, [((N_SP, 1, CHUNK), f32)], flops=3 * 10 ** 8, moved=2 * 10 ** 6,
    )(count, parts, weight, basis, values, index)[0]


def stage_from_rows(recv, phase, rows, amp, direction, gradient):
    return call(
        from_rows, [VMEM] * 6,
        [((LOCAL_M, LOCAL_KB, 2 * KA), f32), ((SIDE, 128), f32)],
        flops=10 ** 8, moved=10 ** 6,
    )(recv, phase, rows, amp, direction, gradient)


def stage_update(parts, control, gradient, direction, product):
    shape = (LOCAL_M, LOCAL_KB, 2 * KA)
    return call(
        update, [VMEM] * 5, [(shape, f32)] * 3, flops=10 ** 5, moved=10 ** 5,
    )(parts, control, gradient, direction, product)


def swap(x):
    return lax.all_to_all(x, "sp", 0, 0, tiled=True)


def shards(phase, rows, control, gradient, direction, perturb, obs_index, obs_count, obs_weight, cutoff):
    pencil = lax.axis_index("sp").astype(i32).reshape(1)
    send, amp = stage_to_rows(cutoff, pencil, direction, phase, rows)
    basis, values = stage_at_slots(obs_index, perturb.reshape(LOCAL_M * LEVELS * ROWS, NB))
    part = stage_sample(swap(send), basis, values, obs_index)
    parts = lax.all_gather(part, "mem")
    send = stage_spread(obs_count, parts, obs_weight, basis, values, obs_index)
    product, sums = stage_from_rows(swap(send), phase, rows, amp, direction, gradient)
    sums = jnp.sum(lax.all_gather(sums, "mem"), axis=0)
    sums = lax.all_gather(sums, "sp")
    return tuple(stage_update(sums, control, gradient, direction, product))


def solution(mesh):
    spectral = P("mem", "sp", None)
    placed = (spectral, spectral, spectral, P("mem", None, "sp", None), P("sp", None), P("sp"), P("sp", None), P())
    phase, rows = tables()
    return jax.shard_map(
        functools.partial(shards, phase, rows),
        mesh=mesh,
        in_specs=placed,
        out_specs=(spectral, spectral, spectral),
        check_vma=False,
    )
```

time: 472 us -> 128 us (0.27)
  the two profiles are of different devices: /device:TPU:1 before, /device:TPU:2 now
where the time goes in v1:
time: 128 us
  blocking collectives  91.5 us (71%)
  starting transfers between devices  16.6 us (13%)
  Pallas kernels  9.77 us (8%)
  waiting for transfers between devices  6.17 us (5%)
  between operations  2.04 us (2%)
  local copies, waits for them, and re-layouts  1.8 us (1%)
    all_gather x1, blocking collectives, shards(): sums = lax.all_gather(sums, 'sp')  46.9 us
    all_to_all x1, blocking collectives, swap(): return lax.all_to_all(x, 'sp', 0, 0, tiled=True)  18.9 us
    all_to_all x1, starting transfers between devices, swap(): return lax.all_to_all(x, 'sp', 0, 0, tiled=True)  16.6 us
    all_gather x1, blocking collectives, shards(): parts = lax.all_gather(part, 'mem')  12.8 us
    all_gather x1, blocking collectives, shards(): sums = jnp.sum(lax.all_gather(sums, 'mem'), axis=0)  12.8 us
    all_to_all x1, waiting for transfers between devices, swap(): return lax.all_to_all(x, 'sp', 0, 0, tiled=True)  6.17 us
    pallas_call x1, Pallas kernels, stage_at_slots(): call(at_slots, [VMEM, VMEM], [((2, 2 * KB, SLOTS), bf16), ((LOCAL_M, SLOT...  3.83 us
    pallas_call x1, Pallas kernels, stage_to_rows(): call(to_rows, [SMEM, SMEM, HBM, HBM, HBM], [((N_SP, 1, CHUNK), f32), ((LO...  2.7 us
  transfers between devices with their start and end apart: 1, of which 1 were waited for; matrix products, arithmetic and copies ran while one was open for 0% of the time, Pallas kernels for 3%

profile of v1, /device:TPU:2, one launch (start us, length us, event | category | flops | bytes accessed | tf_op | source)
XLA Modules:
  0.0 127.8 jit_solution(11764215636777471028)
XLA Ops:
  1.3 2.7 %shard_map.121 = (f32[64,1,384]{2,1,0:T(1,128)}, f32[4,512]{1,0:T(4,128)}) custom-call(s32[1]{0:T(128)S(6)} %copy.14.cut_ref, s32[1]{0:T(128)} %bitcast.pen_ref, f32[2,4,512]{2,1,0:T(4,128)} %dir_ref.3, f32[2,64,256]{2,1,0:T(8,128)} %constant.10.clone.phase_in.phase_ref, bf16[2,48,512]{2,1,0:T(8,128)(2,1)} %constant.11.clone.rows_in.rows_ref), custom_call_target="tpu_custom_call" | custom-call | flops 100000000 | bytes 1000000 | tf_op jit(solution)/shard_map/pallas_call | solution.py:258
  4.0 16.6 %all-to-all-start = ((f32[64,1,384]{2,1,0:T(1,128)}), f32[64,1,384]{2,1,0:T(1,128)S(1)}, u32[]{:S(2)}, u32[]{:S(2)}) async-start(f32[64,1,384]{2,1,0:T(1,128)} %get-tuple-element.9), calls=%async_computation | async-start | bytes 196608 | tf_op jit(solution)/shard_map/all_to_all | solution.py:304
  21.2 0.0 copy-start
  21.3 0.7 copy-done
  21.9 0.0 copy-start.6
  21.9 1.1 copy-done.6
  23.0 0.0 copy-start.1
  23.0 3.8 %shard_map.122 = (bf16[2,256,2048]{2,1,0:T(8,128)(2,1)S(1)}, f32[2,2048]{1,0:T(2,128)S(1)}) custom-call(s32[1,2048]{1,0:T(1,128)S(1)} %copy-done, bf16[192,1536]{1,0:T(8,128)(2,1)S(1)} %bitcast.8), custom_call_target="tpu_custom_call" | custom-call | flops 2000000000 | bytes 4000000 | tf_op jit(solution)/shard_map/pallas_call | solution.py:269
  26.9 0.0 copy-start.5
  26.9 6.2 %all-to-all-done.recv_ref = f32[64,1,384]{2,1,0:T(1,128)S(1)} async-done(((f32[64,1,384]{2,1,0:T(1,128)}), f32[64,1,384]{2,1,0:T(1,128)S(1)}, u32[]{:S(2)}, u32[]{:S(2)}) %all-to-all-start) | async-done | bytes 98336 | tf_op jit(solution)/shard_map/all_to_all | solution.py:304
  33.0 0.0 copy-done.1
  33.0 0.0 copy-start.2
  33.0 0.0 copy-start.3
  33.0 0.0 copy-start.7
  33.1 0.0 copy-start.8
  33.1 0.0 copy-start.9
  33.1 0.7 shard_map.123
  33.8 0.0 copy-start.4
  33.8 12.8 %all-gather.3.parts_ref = f32[8,1,2048]{2,1,0:T(1,128)S(1)} all-gather(f32[1,1,2048]{2,1,0:T(1,128)S(1)} %bitcast.7), channel_id=2, replica_groups=mesh['mem'=8,'sp'=64] {'mem'}, dimensions={0}, use_global_device_ids=true | all-gather | bytes 73728 | tf_op jit(solution)/shard_map/all_gather | solution.py:312
  46.6 0.0 copy-done.5
  46.6 1.0 shard_map.124
  47.6 18.9 %all_to_all.10.recv_ref = f32[64,1,384]{2,1,0:T(1,128)S(1)} all-to-all(f32[64,1,384]{2,1,0:T(1,128)S(1)} %shard_map.124), channel_id=1, replica_groups=mesh['mem'=8,'sp'=64] {'sp'}, dimensions={0} | all-to-all | bytes 196608 | tf_op jit(solution)/shard_map/all_to_all | solution.py:304
  66.5 0.0 copy-done.2
  66.5 0.0 copy-done.3
  66.5 0.0 copy-done.7
  66.5 0.0 copy-done.8
  66.5 0.0 copy-done.9
  66.5 0.7 shard_map.125
  67.3 12.8 %all-gather.1 = f32[64,128]{1,0:T(8,128)S(1)} all-gather(f32[8,128]{1,0:T(8,128)S(1)} %get-tuple-element.13), channel_id=3, replica_groups=mesh['mem'=8,'sp'=64] {'mem'}, dimensions={0}, use_global_device_ids=true | all-gather | bytes 36864 | tf_op jit(solution)/shard_map/all_gather | solution.py:315
  80.1 46.9 %all-gather.2 = f32[512,128]{1,0:T(8,128)S(1)} all-gather(f32[8,128]{1,0:T(8,128)S(1)} %bitcast_reduce_fusion), channel_id=4, replica_groups=mesh['mem'=8,'sp'=64] {'sp'}, dimensions={0}, use_global_device_ids=true | all-gather | bytes 266240 | tf_op jit(solution)/shard_map/all_gather | solution.py:316
  127.0 0.0 copy-done.4
  127.0 0.8 shard_map.126
  (1 shorter events, 0.0 us)
Async XLA Ops:
  4.0 29.0 %all-to-all-start = ((f32[64,1,384]{2,1,0:T(1,128)}), f32[64,1,384]{2,1,0:T(1,128)S(1)}, u32[]{:S(2)}, u32[]{:S(2)}) async-start(f32[64,1,384]{2,1,0:T(1,128)} %get-tuple-element.9), calls=%async_computation | async-start | bytes 196608 | tf_op jit(solution)/shard_map/all_to_all | solution.py:304
  21.2 0.7 copy-start
  21.9 1.1 copy-start.6
  23.0 10.0 %copy-start.1 = (s32[1,2048]{1,0:T(1,128)S(1)}, s32[1,2048]{1,0:T(1,128)}, u32[]{:S(2)}) copy-start(s32[1,2048]{1,0:T(1,128)} %index_ref.5) | copy-start | bytes 24580
  26.9 19.7 %copy-start.5 = (f32[1,2048]{1,0:T(1,128)S(1)}, f32[1,2048]{1,0:T(1,128)}, u32[]{:S(2)}) copy-start(f32[1,2048]{1,0:T(1,128)} %weight_ref.1) | copy-start | bytes 24580
  33.0 33.5 %copy-start.2 = (f32[2,4,512]{2,1,0:T(4,128)S(1)}, f32[2,4,512]{2,1,0:T(4,128)}, u32[]{:S(2)}) copy-start(f32[2,4,512]{2,1,0:T(4,128)} %dir_ref.3) | copy-start | bytes 49156
  33.0 33.5 %copy-start.3 = (f32[2,4,512]{2,1,0:T(4,128)S(1)}, f32[2,4,512]{2,1,0:T(4,128)}, u32[]{:S(2)}) copy-start(f32[2,4,512]{2,1,0:T(4,128)} %grad_ref.3) | copy-start | bytes 49156
  33.0 33.5 %copy-start.7 = (f32[2,64,256]{2,1,0:T(8,128)S(1)}, f32[2,64,256]{2,1,0:T(8,128)}, u32[]{:S(2)}) copy-start(f32[2,64,256]{2,1,0:T(8,128)} %constant.10.clone.phase_in.phase_ref) | copy-start | bytes 393220
  33.1 33.5 %copy-start.8 = (bf16[2,48,512]{2,1,0:T(8,128)(2,1)S(1)}, bf16[2,48,512]{2,1,0:T(8,128)(2,1)}, u32[]{:S(2)}) copy-start(bf16[2,48,512]{2,1,0:T(8,128)(2,1)} %constant.11.clone.rows_in.rows_ref) | copy-start | bytes 294916
  33.1 33.5 %copy-start.9 = (f32[4,512]{1,0:T(4,128)S(1)}, f32[4,512]{1,0:T(4,128)}, u32[]{:S(2)}) copy-start(f32[4,512]{1,0:T(4,128)} %get-tuple-element.12.amp_ref) | copy-start | bytes 24580
  33.8 93.3 %copy-start.4 = (f32[2,4,512]{2,1,0:T(4,128)S(1)}, f32[2,4,512]{2,1,0:T(4,128)}, u32[]{:S(2)}) copy-start(f32[2,4,512]{2,1,0:T(4,128)} %cont_ref.1) | copy-start | bytes 49156

commit v2 on v1

--- a/solution.py
+++ b/solution.py
@@ -33,10 +33,8 @@
     cos_rows = np.cos(2.0 * np.pi * ((r * w) % NA) / NA)
     sin_rows = np.sin(2.0 * np.pi * ((r * ws) % NA) / NA)
     rows = np.concatenate([cos_rows, sin_rows], axis=1).astype(np.float32)
-    high = rows.astype(jnp.bfloat16)
-    low = (rows - high.astype(np.float32)).astype(jnp.bfloat16)
     phase = np.stack([np.cos(turn), np.sin(turn)]).astype(np.float32)
-    return phase, np.stack([high, low])
+    return phase, rows
 
 
 def split(x):
@@ -58,12 +56,17 @@
     return jnp.where(retained, factor, 0.0)
 
 
-def to_rows(cut_ref, pen_ref, dir_in, phase_in, rows_in, out_ref, amp_ref, high_ref, low_ref, dir_ref, phase_ref,
-            rows_ref, sems):
-    pairs = ((dir_in, dir_ref), (phase_in, phase_ref), (rows_in, rows_ref))
-    copies = [pltpu.make_async_copy(a, b, sems.at[i]) for i, (a, b) in enumerate(pairs)]
-    for copy in copies:
-        copy.start()
+def to_rows(pen_ref, cut_ref, dir_in, out_ref, amp_ref, high_ref, low_ref, dir_ref, sem):
+    dir_copy = pltpu.make_async_copy(dir_in, dir_ref, sem)
+    dir_copy.start()
+    w = lax.broadcasted_iota(i32, (1, KA), 1)
+    s = lax.broadcasted_iota(i32, (N_SP, 1), 0)
+    phase_c, phase_s = turns_to_cos_sin(((s * w) & (N_SP - 1)).astype(f32) * (1.0 / N_SP))
+    r = lax.broadcasted_iota(i32, (ROWS, 1), 0)
+    slot = lax.broadcasted_iota(i32, (1, 2 * KA), 1)
+    ws = jnp.where(slot < KA, slot, jnp.where(slot == KA, KA, slot - KA))
+    cos_r, sin_r = turns_to_cos_sin(residue_turns(ws.astype(f32), r.astype(f32), NA))
+    table_high, table_low = split(jnp.where(slot < KA, cos_r, sin_r))
     cutoff, pencil = cut_ref[0], pen_ref[0]
     wa = lax.broadcasted_iota(i32, (1, 384), 1)
     wb = lax.broadcasted_iota(i32, (136, 1), 0)
@@ -78,9 +81,7 @@
     amp = shape_factor(wa * wa + 4 * (wb * wb), cutoff) * gain
     amp_ref[...] = amp
 
-    for copy in copies:
-        copy.wait()
-    phase_c, phase_s = phase_ref[0], phase_ref[1]
+    dir_copy.wait()
     for m in range(LOCAL_M):
         spectral = amp * dir_ref[m]
         part_c = spectral[:, :KA]
@@ -93,8 +94,8 @@
                 high_ref[at, half * KA:(half + 1) * KA] = high
                 low_ref[at, half * KA:(half + 1) * KA] = low
     nt = ((1,), (1,))
-    result = (dot(high_ref[...], rows_ref[0], nt) + dot(high_ref[...], rows_ref[1], nt)
-              + dot(low_ref[...], rows_ref[0], nt))
+    result = (dot(high_ref[...], table_high, nt) + dot(high_ref[...], table_low, nt)
+              + dot(low_ref[...], table_high, nt))
     for i in range(LOCAL_M * LOCAL_KB):
         out_ref[:, 0, i * ROWS:(i + 1) * ROWS] = result[i * N_SP:(i + 1) * N_SP]
 
@@ -119,13 +120,15 @@
     return jnp.where((q == 1) | (q == 2), -cos, cos), jnp.where(q >= 2, -sin, sin)
 
 
-def residue_turns(wavenum, column):
-    product = wavenum * column
-    return (product - jnp.floor(product * (1.0 / NB)) * NB) * (1.0 / NB)
-
-
-def at_slots(index_ref, pert_ref, basis_ref, values_ref):
+def residue_turns(wavenum, place, length):
+    product = wavenum * place
+    return (product - jnp.floor(product * (1.0 / length)) * length) * (1.0 / length)
+
+
+def at_slots(count_ref, index_ref, weight_ref, pert_ref, basis_ref, values_ref, masked_ref):
     block = 256
+    usable = lax.broadcasted_iota(i32, (1, SLOTS), 1) < count_ref[0]
+    masked_ref[...] = jnp.where(usable, weight_ref[...] * (SCALE * SCALE), 0.0)
 
     @pl.loop(0, SLOTS // block)
     def _(step):
@@ -135,11 +138,11 @@
         column = index - line * NB
         place = column.astype(f32)
         y = lax.broadcasted_iota(i32, (SIDE, 1), 0)
-        cos_y, sin_y = turns_to_cos_sin(residue_turns((4 * y).astype(f32), place))
+        cos_y, sin_y = turns_to_cos_sin(residue_turns((4 * y).astype(f32), place, NB))
         q = lax.broadcasted_iota(i32, (SIDE * LOCAL_KB, 1), 0)
         is_sin = (q & 7) >= SIDE // 2
         wq = (32 * (q & 3) + (q >> 3) + is_sin.astype(i32)).astype(f32)
-        cos_q, sin_q = turns_to_cos_sin(residue_turns(wq, place) - jnp.where(is_sin, 0.25, 0.0))
+        cos_q, sin_q = turns_to_cos_sin(residue_turns(wq, place, NB) - jnp.where(is_sin, 0.25, 0.0))
         for pair in range(SIDE * LOCAL_KB // 2):
             both = [cos_y * cos_q[g:g + 1] - sin_y * sin_q[g:g + 1] for g in (2 * pair, 2 * pair + 1)]
             high, low = split(jnp.concatenate(both, axis=0))
@@ -169,13 +172,13 @@
     for m in range(LOCAL_M):
         part = jnp.sum(jnp.where(mine, rows[m * ROWS:(m + 1) * ROWS], 0.0), axis=0, keepdims=True)
         total += values_ref[m:m + 1] * part
-    out_ref[...] = total * SCALE
-
-
-def spread(count_ref, parts_ref, weight_ref, basis_ref, values_ref, index_ref, out_ref):
+    out_ref[...] = jnp.concatenate([total[:, i * 128:(i + 1) * 128] for i in range(SLOTS // 128)], axis=0)
+
+
+def spread(parts_ref, masked_ref, basis_ref, values_ref, index_ref, out_ref):
     sampled = jnp.sum(parts_ref[...], axis=0)
-    usable = lax.broadcasted_iota(i32, (1, SLOTS), 1) < count_ref[0]
-    weighted = jnp.where(usable, weight_ref[...] * sampled, 0.0) * SCALE
+    sampled = jnp.concatenate([sampled[i:i + 1] for i in range(SLOTS // 128)], axis=1)
+    weighted = masked_ref[...] * sampled
     line, _ = cell_parts(index_ref)
     row = jnp.where(line >= ROWS, line - ROWS, line)
     mine = lax.broadcasted_iota(i32, (ROWS, SLOTS), 0) == row
@@ -205,7 +208,8 @@
     left = jnp.concatenate([recv_ref[:, 0, i * ROWS:(i + 1) * ROWS] for i in range(count)], axis=0)
     high, low = split(left)
     nn = ((1,), (0,))
-    turned = dot(high, rows_ref[0], nn) + dot(high, rows_ref[1], nn) + dot(low, rows_ref[0], nn)
+    table_high, table_low = split(rows_ref[...])
+    turned = dot(high, table_high, nn) + dot(high, table_low, nn) + dot(low, table_high, nn)
     phase_c, phase_s = phase_ref[0], phase_ref[1]
     amp = amp_ref[...]
     totals = [jnp.zeros((1, 128), f32)] * 4
@@ -223,13 +227,20 @@
         prod_ref[m] = product
         terms = (g * g, d * product, g * product, product * product)
         totals = [t + fold(x) for t, x in zip(totals, terms)]
-    sums = jnp.concatenate(totals + [jnp.zeros((4, 128), f32)], axis=0)
-    sums_ref[...] = sums
+    lane = lax.broadcasted_iota(i32, (1, 128), 1)
+    line = jnp.zeros((1, 128), f32)
+    for k, t in enumerate(totals):
+        t = t + pltpu.roll(t, 64, 1)
+        t = t + pltpu.roll(t, 32, 1)
+        line = jnp.where((lane >> 5) == k, t, line)
+    sums_ref[...] = line
 
 
 def update(parts_ref, cont_ref, grad_ref, dir_ref, prod_ref, cont_out, grad_out, dir_out):
-    sums = jnp.sum(jnp.sum(parts_ref[...], axis=0), axis=1, keepdims=True)
-    grad_sq, curvature, cross, prod_sq = [sums[i:i + 1] for i in range(4)]
+    line = jnp.sum(parts_ref[...], axis=0)
+    group = lax.broadcasted_iota(i32, (1, 128), 1) >> 5
+    grad_sq, curvature, cross, prod_sq = [
+        jnp.sum(jnp.where(group == k, line, 0.0), axis=1, keepdims=True) for k in range(4)]
     step = grad_sq / curvature
     new_sq = grad_sq + step * (2.0 * cross + step * prod_sq)
     ratio = new_sq / grad_sq
@@ -254,41 +265,40 @@
     )
 
 
-def stage_to_rows(cutoff, pencil, direction, phase, rows):
-    return call(
-        to_rows, [SMEM, SMEM, HBM, HBM, HBM],
+def stage_to_rows(pencil, cutoff, direction):
+    return call(
+        to_rows, [SMEM, SMEM, HBM],
         [((N_SP, 1, CHUNK), f32), ((LOCAL_KB, 2 * KA), f32)],
         [pltpu.VMEM((8 * N_SP, 2 * KA), bf16), pltpu.VMEM((8 * N_SP, 2 * KA), bf16),
-         pltpu.VMEM((LOCAL_M, LOCAL_KB, 2 * KA), f32), pltpu.VMEM((2, N_SP, KA), f32),
-         pltpu.VMEM((2, ROWS, 2 * KA), bf16), pltpu.SemaphoreType.DMA((3,))],
+         pltpu.VMEM((LOCAL_M, LOCAL_KB, 2 * KA), f32), pltpu.SemaphoreType.DMA],
         flops=10 ** 8, moved=10 ** 6, params=WHOLE,
-    )(cutoff, pencil, direction, phase, rows)
-
-
-def stage_at_slots(index, perturb):
-    return call(
-        at_slots, [VMEM, VMEM],
-        [((2, 2 * KB, SLOTS), bf16), ((LOCAL_M, SLOTS), f32)],
+    )(pencil, cutoff, direction)
+
+
+def stage_at_slots(count, index, weight, perturb):
+    return call(
+        at_slots, [SMEM] + [VMEM] * 3,
+        [((2, 2 * KB, SLOTS), bf16), ((LOCAL_M, SLOTS), f32), ((1, SLOTS), f32)],
         flops=2 * 10 ** 9, moved=4 * 10 ** 6,
-    )(index, perturb)
+    )(count, index, weight, perturb)
 
 
 def stage_sample(recv, basis, values, index):
     return call(
-        sample, [VMEM] * 4, [((1, SLOTS), f32)], flops=3 * 10 ** 8, moved=2 * 10 ** 6,
+        sample, [VMEM] * 4, [((SLOTS // 128, 128), f32)], flops=3 * 10 ** 8, moved=2 * 10 ** 6,
     )(recv, basis, values, index)[0]
 
 
-def stage_spread(count, parts, weight, basis, values, index):
-    return call(
-        spread, [SMEM] + [VMEM] * 5, [((N_SP, 1, CHUNK), f32)], flops=3 * 10 ** 8, moved=2 * 10 ** 6,
-    )(count, parts, weight, basis, values, index)[0]
+def stage_spread(parts, masked, basis, values, index):
+    return call(
+        spread, [VMEM] * 5, [((N_SP, 1, CHUNK), f32)], flops=3 * 10 ** 8, moved=2 * 10 ** 6,
+    )(parts, masked, basis, values, index)[0]
 
 
 def stage_from_rows(recv, phase, rows, amp, direction, gradient):
     return call(
         from_rows, [VMEM] * 6,
-        [((LOCAL_M, LOCAL_KB, 2 * KA), f32), ((SIDE, 128), f32)],
+        [((LOCAL_M, LOCAL_KB, 2 * KA), f32), ((1, 128), f32)],
         flops=10 ** 8, moved=10 ** 6,
     )(recv, phase, rows, amp, direction, gradient)
 
@@ -300,20 +310,29 @@
     )(parts, control, gradient, direction, product)
 
 
+NEAR = [[m * N_SP + s + y for m in range(SIDE) for y in range(4)] for s in range(0, N_SP, 4)]
+FAR = [[m * N_SP + s + y for s in range(0, N_SP, 4)] for m in range(SIDE) for y in range(4)]
+
+
 def swap(x):
     return lax.all_to_all(x, "sp", 0, 0, tiled=True)
 
 
+def share(x, axis, count, groups=None):
+    x = jnp.broadcast_to(x[None], (count,) + x.shape)
+    return lax.all_to_all(x, axis, 0, 0, axis_index_groups=groups, tiled=True)
+
+
 def shards(phase, rows, control, gradient, direction, perturb, obs_index, obs_count, obs_weight, cutoff):
     pencil = lax.axis_index("sp").astype(i32).reshape(1)
-    send, amp = stage_to_rows(cutoff, pencil, direction, phase, rows)
-    basis, values = stage_at_slots(obs_index, perturb.reshape(LOCAL_M * LEVELS * ROWS, NB))
+    send, amp = stage_to_rows(pencil, cutoff, direction)
+    basis, values, masked = stage_at_slots(
+        obs_count, obs_index, obs_weight, perturb.reshape(LOCAL_M * LEVELS * ROWS, NB))
     part = stage_sample(swap(send), basis, values, obs_index)
-    parts = lax.all_gather(part, "mem")
-    send = stage_spread(obs_count, parts, obs_weight, basis, values, obs_index)
+    send = stage_spread(share(part, "mem", SIDE), masked, basis, values, obs_index)
     product, sums = stage_from_rows(swap(send), phase, rows, amp, direction, gradient)
-    sums = jnp.sum(lax.all_gather(sums, "mem"), axis=0)
-    sums = lax.all_gather(sums, "sp")
+    sums = jnp.sum(share(sums, ("mem", "sp"), len(NEAR[0]), NEAR), axis=0)
+    sums = share(sums, ("mem", "sp"), len(FAR[0]), FAR)
     return tuple(stage_update(sums, control, gradient, direction, product))
 
 

time: 128 us -> 92.8 us (0.72)
  the two profiles are of different devices: /device:TPU:2 before, /device:TPU:1 now
where the time goes in v2:
time: 92.8 us; the launch traced here: 92.3 us
  blocking collectives  56.6 us (61%)
  starting transfers between devices  17.1 us (18%)
  Pallas kernels  9.53 us (10%)
  waiting for transfers between devices  4.42 us (5%)
  local copies, waits for them, and re-layouts  2.51 us (3%)
  between operations  2.04 us (2%)
    all_to_all x3, blocking collectives, share(): return lax.all_to_all(x, axis, 0, 0, axis_index_groups=groups, tiled=True)  38.5 us
    all_to_all x1, blocking collectives, swap(): return lax.all_to_all(x, 'sp', 0, 0, tiled=True)  18.1 us
    all_to_all x1, starting transfers between devices, swap(): return lax.all_to_all(x, 'sp', 0, 0, tiled=True)  17.1 us
    all_to_all x1, waiting for transfers between devices, swap(): return lax.all_to_all(x, 'sp', 0, 0, tiled=True)  4.42 us
    pallas_call x1, Pallas kernels, stage_at_slots(): call(at_slots, [SMEM] + [VMEM] * 3, [((2, 2 * KB, SLOTS), bf16), ((LOCAL_...  3.86 us
    unnamed x20, local copies, waits for them, and re-layouts  2.49 us
    pallas_call x1, Pallas kernels, stage_to_rows(): call(to_rows, [SMEM, SMEM, HBM], [((N_SP, 1, CHUNK), f32), ((LOCAL_KB, 2...  2.43 us
  transfers between devices with their start and end apart: 1, of which 1 were waited for; matrix products, arithmetic and copies ran while one was open for 0% of the time, Pallas kernels for 4%

profile of v2, /device:TPU:1, one launch (start us, length us, event | category | flops | bytes accessed | tf_op | source)
XLA Modules:
  0.0 92.3 jit_solution(533043313741117894)
XLA Ops:
  1.3 2.4 %shard_map.121 = (f32[64,1,384]{2,1,0:T(1,128)}, f32[4,512]{1,0:T(4,128)}) custom-call(s32[1]{0:T(128)} %bitcast.pen_ref, s32[1]{0:T(128)S(6)} %copy.15.cut_ref, f32[2,4,512]{2,1,0:T(4,128)} %dir_ref.3), custom_call_target="tpu_custom_call" | custom-call | flops 100000000 | bytes 1000000 | tf_op jit(solution)/shard_map/pallas_call | solution.py:269
  3.7 17.1 %all-to-all-start = ((f32[64,1,384]{2,1,0:T(1,128)}), f32[64,1,384]{2,1,0:T(1,128)S(1)}, u32[]{:S(2)}, u32[]{:S(2)}) async-start(f32[64,1,384]{2,1,0:T(1,128)} %get-tuple-element.10), calls=%async_computation | async-start | bytes 196608 | tf_op jit(solution)/shard_map/all_to_all | solution.py:318
  21.5 0.0 copy-start
  21.5 0.7 copy-done
  22.2 0.0 copy-start.5
  22.2 1.1 %copy-done.5 = bf16[2,2,48,1536]{3,2,1,0:T(8,128)(2,1)S(1)} copy-done((bf16[2,2,48,1536]{3,2,1,0:T(8,128)(2,1)S(1)}, bf16[2,2,48,1536]{3,2,1,0:T(8,128)(2,1)}, u32[]{:S(2)}) %copy-start.5) | copy-done | bytes 589848
  23.3 0.0 copy-start.6
  23.3 0.7 copy-done.6
  24.0 0.0 copy-start.1
  24.0 3.9 %shard_map.122 = (bf16[2,256,2048]{2,1,0:T(8,128)(2,1)S(1)}, f32[2,2048]{1,0:T(2,128)S(1)}, f32[1,2048]{1,0:T(1,128)S(1)}) custom-call(s32[1]{0:T(128)S(6)} %copy.14.count_ref, s32[1,2048]{1,0:T(1,128)S(1)} %copy-done, f32[1,2048]{1,0:T(1,128)S(1)} %copy-done.6, bf16[192,1536]{1,0:T(8,128)(2,1)S(1)} %bitcast.5), custom_call_target="tpu_custom_call" | custom-call | flops 2000000000 | bytes 4000000 | tf_op jit(solution)/shard_map/pallas_call | solution.py:279
  27.8 4.4 %all-to-all-done.recv_ref = f32[64,1,384]{2,1,0:T(1,128)S(1)} async-done(((f32[64,1,384]{2,1,0:T(1,128)}), f32[64,1,384]{2,1,0:T(1,128)S(1)}, u32[]{:S(2)}, u32[]{:S(2)}) %all-to-all-start) | async-done | bytes 98336 | tf_op jit(solution)/shard_map/all_to_all | solution.py:318
  32.3 0.0 copy-done.1
  32.3 0.0 copy-start.2
  32.3 0.0 copy-start.3
  32.3 0.0 copy-start.7
  32.3 0.0 copy-start.8
  32.3 0.0 copy-start.9
  32.3 0.7 shard_map.123
  33.0 0.0 copy-start.4
  33.0 10.9 %all_to_all.25.parts_ref = f32[8,16,128]{2,1,0:T(8,128)S(1)} all-to-all(f32[8,16,128]{2,1,0:T(8,128)S(1)} %broadcast_in_dim.8), channel_id=1, replica_groups=mesh['mem'=8,'sp'=64] {'mem'}, dimensions={0} | all-to-all | bytes 131072 | tf_op jit(solution)/shard_map/all_to_all | solution.py:323
  44.0 1.0 %shard_map.124 = f32[64,1,384]{2,1,0:T(1,128)S(1)} custom-call(f32[8,16,128]{2,1,0:T(8,128)S(1)} %all_to_all.25.parts_ref, f32[1,2048]{1,0:T(1,128)S(1)} %get-tuple-element.13.masked_ref, bf16[2,256,2048]{2,1,0:T(8,128)(2,1)S(1)} %get-tuple-element.11.basis_ref, f32[2,2048]{1,0:T(2,128)S(1)} %get-tuple-element.12.values_ref, s32[1,2048]{1,0:T(1,128)S(1)} %copy-done.1), custom_call_target="tpu_custom_call" | custom-call | flops 300000000 | bytes 2000000 | tf_op jit(solution)/shard_map/pallas_call | solution.py:293
  44.9 18.1 %all_to_all.26.recv_ref = f32[64,1,384]{2,1,0:T(1,128)S(1)} all-to-all(f32[64,1,384]{2,1,0:T(1,128)S(1)} %shard_map.124), channel_id=1, replica_groups=mesh['mem'=8,'sp'=64] {'sp'}, dimensions={0} | all-to-all | bytes 196608 | tf_op jit(solution)/shard_map/all_to_all | solution.py:318
  63.0 0.0 copy-done.2
  63.1 0.0 copy-done.3
  63.1 0.0 copy-done.7
  63.1 0.0 copy-done.8
  63.1 0.0 copy-done.9
  63.1 0.9 shard_map.125
  64.0 12.1 %all_to_all.27 = f32[32,1,128]{2,1,0:T(1,128)S(1)} all-to-all(f32[32,1,128]{2,1,0:T(1,128)S(1)} %broadcast_in_dim.10), channel_id=1, replica_groups={{0,1,2,3,64,65,66,67,128,129,130,131,192,193,194,195,256,257,258,259,32..., dimensions={0} | all-to-all | bytes 32768 | tf_op jit(solution)/shard_map/all_to_all | solution.py:323
  76.1 15.4 %all_to_all.28.parts_ref = f32[16,1,128]{2,1,0:T(1,128)S(1)} all-to-all(f32[16,1,128]{2,1,0:T(1,128)S(1)} %broadcast_in_dim.11), channel_id=1, replica_groups={{0,4,8,12,16,20,24,28,32,36,40,44,48,52,56,60},{1,5,9,13,17,21,25,29,33..., dimensions={0} | all-to-all | bytes 16384 | tf_op jit(solution)/shard_map/all_to_all | solution.py:323
  91.6 0.0 copy-done.4
  91.6 0.7 shard_map.126
  (4 shorter events, 0.0 us)
Async XLA Ops:
  3.7 28.5 %all-to-all-start = ((f32[64,1,384]{2,1,0:T(1,128)}), f32[64,1,384]{2,1,0:T(1,128)S(1)}, u32[]{:S(2)}, u32[]{:S(2)}) async-start(f32[64,1,384]{2,1,0:T(1,128)} %get-tuple-element.10), calls=%async_computation | async-start | bytes 196608 | tf_op jit(solution)/shard_map/all_to_all | solution.py:318
  21.5 0.7 copy-start
  22.2 1.1 %copy-start.5 = (bf16[2,2,48,1536]{3,2,1,0:T(8,128)(2,1)S(1)}, bf16[2,2,48,1536]{3,2,1,0:T(8,128)(2,1)}, u32[]{:S(2)}) copy-start(bf16[2,2,48,1536]{3,2,1,0:T(8,128)(2,1)} %param.13) | copy-start | bytes 1769476
  23.3 0.7 copy-start.6
  24.0 8.3 %copy-start.1 = (s32[1,2048]{1,0:T(1,128)S(1)}, s32[1,2048]{1,0:T(1,128)}, u32[]{:S(2)}) copy-start(s32[1,2048]{1,0:T(1,128)} %index_ref.5) | copy-start | bytes 24580
  32.3 30.8 %copy-start.2 = (f32[2,4,512]{2,1,0:T(4,128)S(1)}, f32[2,4,512]{2,1,0:T(4,128)}, u32[]{:S(2)}) copy-start(f32[2,4,512]{2,1,0:T(4,128)} %dir_ref.3) | copy-start | bytes 49156
  32.3 30.8 %copy-start.3 = (f32[2,4,512]{2,1,0:T(4,128)S(1)}, f32[2,4,512]{2,1,0:T(4,128)}, u32[]{:S(2)}) copy-start(f32[2,4,512]{2,1,0:T(4,128)} %grad_ref.3) | copy-start | bytes 49156
  32.3 30.8 %copy-start.7 = (f32[2,64,256]{2,1,0:T(8,128)S(1)}, f32[2,64,256]{2,1,0:T(8,128)}, u32[]{:S(2)}) copy-start(f32[2,64,256]{2,1,0:T(8,128)} %constant.10.clone.phase_ref) | copy-start | bytes 393220
  32.3 30.8 %copy-start.8 = (f32[48,512]{1,0:T(8,128)S(1)}, f32[48,512]{1,0:T(8,128)}, u32[]{:S(2)}) copy-start(f32[48,512]{1,0:T(8,128)} %constant.11.clone.rows_ref) | copy-start | bytes 294916
  32.3 30.8 %copy-start.9 = (f32[4,512]{1,0:T(4,128)S(1)}, f32[4,512]{1,0:T(4,128)}, u32[]{:S(2)}) copy-start(f32[4,512]{1,0:T(4,128)} %get-tuple-element.14.amp_ref) | copy-start | bytes 24580
  33.0 58.6 %copy-start.4 = (f32[2,4,512]{2,1,0:T(4,128)S(1)}, f32[2,4,512]{2,1,0:T(4,128)}, u32[]{:S(2)}) copy-start(f32[2,4,512]{2,1,0:T(4,128)} %cont_ref.1) | copy-start | bytes 49156

commit v3 on v2

--- a/solution.py
+++ b/solution.py
@@ -96,8 +96,8 @@
     nt = ((1,), (1,))
     result = (dot(high_ref[...], table_high, nt) + dot(high_ref[...], table_low, nt)
               + dot(low_ref[...], table_high, nt))
-    for i in range(LOCAL_M * LOCAL_KB):
-        out_ref[:, 0, i * ROWS:(i + 1) * ROWS] = result[i * N_SP:(i + 1) * N_SP]
+    pieces = [result[i * N_SP:(i + 1) * N_SP] for i in range(LOCAL_M * LOCAL_KB)]
+    out_ref[:, 0, :] = jnp.concatenate(pieces, axis=1)
 
 
 def cell_parts(index_ref):
@@ -160,7 +160,8 @@
 
 def sample(recv_ref, basis_ref, values_ref, index_ref, out_ref):
     wide = LOCAL_M * ROWS
-    field = jnp.concatenate([recv_ref[:, 0, k * wide:(k + 1) * wide] for k in range(LOCAL_KB)], axis=0)
+    recv = recv_ref[:, 0, :]
+    field = jnp.concatenate([recv[:, k * wide:(k + 1) * wide] for k in range(LOCAL_KB)], axis=0)
     high, low = split(field.T)
     nn = ((1,), (0,))
     both = dot(jnp.concatenate([high, low], axis=0), basis_ref[0], nn)
@@ -194,8 +195,8 @@
     both = dot(basis_ref[0], right, nt)
     result = both[:, :128] + both[:, 128:] + dot(basis_ref[1], right[:128], nt)
     wide = LOCAL_M * ROWS
-    for k in range(LOCAL_KB):
-        out_ref[:, 0, k * wide:(k + 1) * wide] = result[k * N_SP:(k + 1) * N_SP, :wide]
+    pieces = [result[k * N_SP:(k + 1) * N_SP, :wide] for k in range(LOCAL_KB)]
+    out_ref[:, 0, :] = jnp.concatenate(pieces, axis=1)
 
 
 def fold(x):
@@ -205,7 +206,8 @@
 
 def from_rows(recv_ref, phase_ref, rows_ref, amp_ref, dir_ref, grad_ref, prod_ref, sums_ref):
     count = LOCAL_M * LOCAL_KB
-    left = jnp.concatenate([recv_ref[:, 0, i * ROWS:(i + 1) * ROWS] for i in range(count)], axis=0)
+    recv = recv_ref[:, 0, :]
+    left = jnp.concatenate([recv[:, i * ROWS:(i + 1) * ROWS] for i in range(count)], axis=0)
     high, low = split(left)
     nn = ((1,), (0,))
     table_high, table_low = split(rows_ref[...])
@@ -310,8 +312,8 @@
     )(parts, control, gradient, direction, product)
 
 
-NEAR = [[m * N_SP + s + y for m in range(SIDE) for y in range(4)] for s in range(0, N_SP, 4)]
-FAR = [[m * N_SP + s + y for s in range(0, N_SP, 4)] for m in range(SIDE) for y in range(4)]
+NEAR = [[m * N_SP + s + y for m in range(SIDE) for y in range(2)] for s in range(0, N_SP, 2)]
+FAR = [[m * N_SP + s + y for s in range(0, N_SP, 2)] for m in range(SIDE) for y in range(2)]
 
 
 def swap(x):

time: 92.8 us -> 88.9 us (0.958)
  blocking collectives: 56.6 us -> 53.2 us
    all_to_all x3, blocking collectives: 38.5 us -> 35.1 us  [share(): return lax.all_to_all(x, axis, 0, 0, axis_index_groups=groups, tiled=True)]
where the time goes in v3:
time: 88.9 us; the launch traced here: 88.3 us
  blocking collectives  53.2 us (60%)
  starting transfers between devices  17.1 us (19%)
  Pallas kernels  9.04 us (10%)
  waiting for transfers between devices  4.42 us (5%)
  local copies, waits for them, and re-layouts  2.51 us (3%)
  between operations  2.04 us (2%)
    all_to_all x3, blocking collectives, share(): return lax.all_to_all(x, axis, 0, 0, axis_index_groups=groups, tiled=True)  35.1 us
    all_to_all x1, blocking collectives, swap(): return lax.all_to_all(x, 'sp', 0, 0, tiled=True)  18.1 us
    all_to_all x1, starting transfers between devices, swap(): return lax.all_to_all(x, 'sp', 0, 0, tiled=True)  17.1 us
    all_to_all x1, waiting for transfers between devices, swap(): return lax.all_to_all(x, 'sp', 0, 0, tiled=True)  4.42 us
    pallas_call x1, Pallas kernels, stage_at_slots(): call(at_slots, [SMEM] + [VMEM] * 3, [((2, 2 * KB, SLOTS), bf16), ((LOCAL_...  3.85 us
    unnamed x20, local copies, waits for them, and re-layouts  2.49 us
    pallas_call x1, Pallas kernels, stage_to_rows(): call(to_rows, [SMEM, SMEM, HBM], [((N_SP, 1, CHUNK), f32), ((LOCAL_KB, 2...  2.07 us
  transfers between devices with their start and end apart: 1, of which 1 were waited for; matrix products, arithmetic and copies ran while one was open for 0% of the time, Pallas kernels for 4%

profile of v3, /device:TPU:1, one launch (start us, length us, event | category | flops | bytes accessed | tf_op | source)
XLA Modules:
  0.0 88.3 jit_solution(1366101194272800706)
XLA Ops:
  1.3 2.1 %shard_map.121 = (f32[64,1,384]{2,1,0:T(1,128)}, f32[4,512]{1,0:T(4,128)}) custom-call(s32[1]{0:T(128)} %bitcast.pen_ref, s32[1]{0:T(128)S(6)} %copy.15.cut_ref, f32[2,4,512]{2,1,0:T(4,128)} %dir_ref.3), custom_call_target="tpu_custom_call" | custom-call | flops 100000000 | bytes 1000000 | tf_op jit(solution)/shard_map/pallas_call | solution.py:271
  3.4 17.1 %all-to-all-start = ((f32[64,1,384]{2,1,0:T(1,128)}), f32[64,1,384]{2,1,0:T(1,128)S(1)}, u32[]{:S(2)}, u32[]{:S(2)}) async-start(f32[64,1,384]{2,1,0:T(1,128)} %get-tuple-element.10), calls=%async_computation | async-start | bytes 196608 | tf_op jit(solution)/shard_map/all_to_all | solution.py:320
  21.2 0.0 copy-start
  21.2 0.7 copy-done
  21.9 0.0 copy-start.5
  21.9 1.1 %copy-done.5 = bf16[2,2,48,1536]{3,2,1,0:T(8,128)(2,1)S(1)} copy-done((bf16[2,2,48,1536]{3,2,1,0:T(8,128)(2,1)S(1)}, bf16[2,2,48,1536]{3,2,1,0:T(8,128)(2,1)}, u32[]{:S(2)}) %copy-start.5) | copy-done | bytes 589848
  22.9 0.0 copy-start.6
  22.9 0.7 copy-done.6
  23.6 0.0 copy-start.1
  23.6 3.9 %shard_map.122 = (bf16[2,256,2048]{2,1,0:T(8,128)(2,1)S(1)}, f32[2,2048]{1,0:T(2,128)S(1)}, f32[1,2048]{1,0:T(1,128)S(1)}) custom-call(s32[1]{0:T(128)S(6)} %copy.14.count_ref, s32[1,2048]{1,0:T(1,128)S(1)} %copy-done, f32[1,2048]{1,0:T(1,128)S(1)} %copy-done.6, bf16[192,1536]{1,0:T(8,128)(2,1)S(1)} %bitcast.5), custom_call_target="tpu_custom_call" | custom-call | flops 2000000000 | bytes 4000000 | tf_op jit(solution)/shard_map/pallas_call | solution.py:281
  27.5 4.4 %all-to-all-done.recv_ref = f32[64,1,384]{2,1,0:T(1,128)S(1)} async-done(((f32[64,1,384]{2,1,0:T(1,128)}), f32[64,1,384]{2,1,0:T(1,128)S(1)}, u32[]{:S(2)}, u32[]{:S(2)}) %all-to-all-start) | async-done | bytes 98336 | tf_op jit(solution)/shard_map/all_to_all | solution.py:320
  31.9 0.0 copy-done.1
  31.9 0.0 copy-start.2
  31.9 0.0 copy-start.3
  31.9 0.0 copy-start.7
  31.9 0.0 copy-start.8
  31.9 0.0 copy-start.9
  31.9 0.7 shard_map.123
  32.6 0.0 copy-start.4
  32.7 10.9 %all_to_all.25.parts_ref = f32[8,16,128]{2,1,0:T(8,128)S(1)} all-to-all(f32[8,16,128]{2,1,0:T(8,128)S(1)} %broadcast_in_dim.8), channel_id=1, replica_groups=mesh['mem'=8,'sp'=64] {'mem'}, dimensions={0} | all-to-all | bytes 131072 | tf_op jit(solution)/shard_map/all_to_all | solution.py:325
  43.6 0.8 shard_map.124
  44.4 18.1 %all_to_all.26.recv_ref = f32[64,1,384]{2,1,0:T(1,128)S(1)} all-to-all(f32[64,1,384]{2,1,0:T(1,128)S(1)} %shard_map.124), channel_id=1, replica_groups=mesh['mem'=8,'sp'=64] {'sp'}, dimensions={0} | all-to-all | bytes 196608 | tf_op jit(solution)/shard_map/all_to_all | solution.py:320
  62.5 0.0 copy-done.2
  62.5 0.0 copy-done.3
  62.5 0.0 copy-done.7
  62.5 0.0 copy-done.8
  62.6 0.0 copy-done.9
  62.6 0.9 shard_map.125
  63.4 10.2 %all_to_all.27 = f32[16,1,128]{2,1,0:T(1,128)S(1)} all-to-all(f32[16,1,128]{2,1,0:T(1,128)S(1)} %broadcast_in_dim.10), channel_id=1, replica_groups={{0,1,64,65,128,129,192,193,256,257,320,321,384,385,448,449},{2,3,66,67,..., dimensions={0} | all-to-all | bytes 16384 | tf_op jit(solution)/shard_map/all_to_all | solution.py:325
  73.7 14.0 %all_to_all.28.parts_ref = f32[32,1,128]{2,1,0:T(1,128)S(1)} all-to-all(f32[32,1,128]{2,1,0:T(1,128)S(1)} %broadcast_in_dim.11), channel_id=1, replica_groups={{0,2,4,6,8,10,12,14,16,18,20,22,24,26,28,30,32,34,36,38,40,42,44,46,48,..., dimensions={0} | all-to-all | bytes 32768 | tf_op jit(solution)/shard_map/all_to_all | solution.py:325
  87.6 0.0 copy-done.4
  87.6 0.7 shard_map.126
  (4 shorter events, 0.0 us)
Async XLA Ops:
  3.4 28.5 %all-to-all-start = ((f32[64,1,384]{2,1,0:T(1,128)}), f32[64,1,384]{2,1,0:T(1,128)S(1)}, u32[]{:S(2)}, u32[]{:S(2)}) async-start(f32[64,1,384]{2,1,0:T(1,128)} %get-tuple-element.10), calls=%async_computation | async-start | bytes 196608 | tf_op jit(solution)/shard_map/all_to_all | solution.py:320
  21.2 0.7 copy-start
  21.9 1.1 %copy-start.5 = (bf16[2,2,48,1536]{3,2,1,0:T(8,128)(2,1)S(1)}, bf16[2,2,48,1536]{3,2,1,0:T(8,128)(2,1)}, u32[]{:S(2)}) copy-start(bf16[2,2,48,1536]{3,2,1,0:T(8,128)(2,1)} %param.13) | copy-start | bytes 1769476
  22.9 0.7 copy-start.6
  23.6 8.3 %copy-start.1 = (s32[1,2048]{1,0:T(1,128)S(1)}, s32[1,2048]{1,0:T(1,128)}, u32[]{:S(2)}) copy-start(s32[1,2048]{1,0:T(1,128)} %index_ref.5) | copy-start | bytes 24580
  31.9 30.6 %copy-start.2 = (f32[2,4,512]{2,1,0:T(4,128)S(1)}, f32[2,4,512]{2,1,0:T(4,128)}, u32[]{:S(2)}) copy-start(f32[2,4,512]{2,1,0:T(4,128)} %dir_ref.3) | copy-start | bytes 49156
  31.9 30.6 %copy-start.3 = (f32[2,4,512]{2,1,0:T(4,128)S(1)}, f32[2,4,512]{2,1,0:T(4,128)}, u32[]{:S(2)}) copy-start(f32[2,4,512]{2,1,0:T(4,128)} %grad_ref.3) | copy-start | bytes 49156
  31.9 30.6 %copy-start.7 = (f32[2,64,256]{2,1,0:T(8,128)S(1)}, f32[2,64,256]{2,1,0:T(8,128)}, u32[]{:S(2)}) copy-start(f32[2,64,256]{2,1,0:T(8,128)} %constant.10.clone.phase_ref) | copy-start | bytes 393220
  31.9 30.6 %copy-start.8 = (f32[48,512]{1,0:T(8,128)S(1)}, f32[48,512]{1,0:T(8,128)}, u32[]{:S(2)}) copy-start(f32[48,512]{1,0:T(8,128)} %constant.11.clone.rows_ref) | copy-start | bytes 294916
  31.9 30.6 %copy-start.9 = (f32[4,512]{1,0:T(4,128)S(1)}, f32[4,512]{1,0:T(4,128)}, u32[]{:S(2)}) copy-start(f32[4,512]{1,0:T(4,128)} %get-tuple-element.14.amp_ref) | copy-start | bytes 24580
  32.6 55.0 %copy-start.4 = (f32[2,4,512]{2,1,0:T(4,128)S(1)}, f32[2,4,512]{2,1,0:T(4,128)}, u32[]{:S(2)}) copy-start(f32[2,4,512]{2,1,0:T(4,128)} %cont_ref.1) | copy-start | bytes 49156

commit v4 on v3

--- a/solution.py
+++ b/solution.py
@@ -15,6 +15,19 @@
 SIDE = 8
 SCALE = 1.0 / math.sqrt(MEMBERS - 1)
 CHUNK = LOCAL_KB * LOCAL_M * ROWS
+
+
+def spanned(masks):
+    out = [0]
+    for mask in masks:
+        out += [mask ^ x for x in out]
+    return out
+
+
+ORDER = spanned([63, 45, 44, 37, 16, 58])
+PLACE = [ORDER.index(s) for s in range(N_SP)]
+NEAR = [[s ^ d for d in spanned([449, 385, 192, 1])] for s in range(0, N_SP, 2)]
+FAR = [[m * N_SP + (y ^ d) for d in spanned([62, 46, 52, 54, 6])] for m in range(SIDE) for y in range(2)]
 
 f32, bf16, i32 = jnp.float32, jnp.bfloat16, jnp.int32
 VMEM = pl.BlockSpec(memory_space=pltpu.VMEM)
@@ -40,6 +53,15 @@
 def split(x):
     high = x.astype(bf16)
     return high, (x - high.astype(f32)).astype(bf16)
+
+
+def put_rows(ref, rows):
+    for p, s in enumerate(ORDER):
+        ref[p] = rows[s:s + 1]
+
+
+def get_rows(ref):
+    return jnp.concatenate([ref[p] for p in PLACE], axis=0)
 
 
 def dot(a, b, dims):
@@ -97,7 +119,7 @@
     result = (dot(high_ref[...], table_high, nt) + dot(high_ref[...], table_low, nt)
               + dot(low_ref[...], table_high, nt))
     pieces = [result[i * N_SP:(i + 1) * N_SP] for i in range(LOCAL_M * LOCAL_KB)]
-    out_ref[:, 0, :] = jnp.concatenate(pieces, axis=1)
+    put_rows(out_ref, jnp.concatenate(pieces, axis=1))
 
 
 def cell_parts(index_ref):
@@ -160,7 +182,7 @@
 
 def sample(recv_ref, basis_ref, values_ref, index_ref, out_ref):
     wide = LOCAL_M * ROWS
-    recv = recv_ref[:, 0, :]
+    recv = get_rows(recv_ref)
     field = jnp.concatenate([recv[:, k * wide:(k + 1) * wide] for k in range(LOCAL_KB)], axis=0)
     high, low = split(field.T)
     nn = ((1,), (0,))
@@ -196,7 +218,7 @@
     result = both[:, :128] + both[:, 128:] + dot(basis_ref[1], right[:128], nt)
     wide = LOCAL_M * ROWS
     pieces = [result[k * N_SP:(k + 1) * N_SP, :wide] for k in range(LOCAL_KB)]
-    out_ref[:, 0, :] = jnp.concatenate(pieces, axis=1)
+    put_rows(out_ref, jnp.concatenate(pieces, axis=1))
 
 
 def fold(x):
@@ -206,7 +228,7 @@
 
 def from_rows(recv_ref, phase_ref, rows_ref, amp_ref, dir_ref, grad_ref, prod_ref, sums_ref):
     count = LOCAL_M * LOCAL_KB
-    recv = recv_ref[:, 0, :]
+    recv = get_rows(recv_ref)
     left = jnp.concatenate([recv[:, i * ROWS:(i + 1) * ROWS] for i in range(count)], axis=0)
     high, low = split(left)
     nn = ((1,), (0,))
@@ -312,12 +334,8 @@
     )(parts, control, gradient, direction, product)
 
 
-NEAR = [[m * N_SP + s + y for m in range(SIDE) for y in range(2)] for s in range(0, N_SP, 2)]
-FAR = [[m * N_SP + s + y for s in range(0, N_SP, 2)] for m in range(SIDE) for y in range(2)]
-
-
 def swap(x):
-    return lax.all_to_all(x, "sp", 0, 0, tiled=True)
+    return lax.all_to_all(x, "sp", 0, 0, axis_index_groups=[ORDER], tiled=True)
 
 
 def share(x, axis, count, groups=None):

time: 88.9 us -> 88.7 us (level)
  no operation moved by 1% of the time
where the time goes in v4:
time: 88.7 us; the launch traced here: 88.2 us
  blocking collectives  53.6 us (60%)
  starting transfers between devices  17.1 us (19%)
  Pallas kernels  9.04 us (10%)
  waiting for transfers between devices  3.8 us (4%)
  local copies, waits for them, and re-layouts  2.51 us (3%)
  between operations  2.04 us (2%)
    all_to_all x3, blocking collectives, share(): return lax.all_to_all(x, axis, 0, 0, axis_index_groups=groups, tiled=True)  35.7 us
    all_to_all x1, blocking collectives, swap(): return lax.all_to_all(x, 'sp', 0, 0, axis_index_groups=[ORDER], tiled=True)  17.9 us
    all_to_all x1, starting transfers between devices, swap(): return lax.all_to_all(x, 'sp', 0, 0, axis_index_groups=[ORDER], tiled=True)  17.1 us
    pallas_call x1, Pallas kernels, stage_at_slots(): call(at_slots, [SMEM] + [VMEM] * 3, [((2, 2 * KB, SLOTS), bf16), ((LOCAL_...  3.85 us
    all_to_all x1, waiting for transfers between devices, swap(): return lax.all_to_all(x, 'sp', 0, 0, axis_index_groups=[ORDER], tiled=True)  3.8 us
    unnamed x20, local copies, waits for them, and re-layouts  2.49 us
    pallas_call x1, Pallas kernels, stage_to_rows(): call(to_rows, [SMEM, SMEM, HBM], [((N_SP, 1, CHUNK), f32), ((LOCAL_KB, 2...  2.07 us
  transfers between devices with their start and end apart: 1, of which 1 were waited for; matrix products, arithmetic and copies ran while one was open for 0% of the time, Pallas kernels for 4%

profile of v4, /device:TPU:1, one launch (start us, length us, event | category | flops | bytes accessed | tf_op | source)
XLA Modules:
  0.0 88.2 jit_solution(6614055938344859543)
XLA Ops:
  1.3 2.1 %shard_map.121 = (f32[64,1,384]{2,1,0:T(1,128)}, f32[4,512]{1,0:T(4,128)}) custom-call(s32[1]{0:T(128)} %bitcast.pen_ref, s32[1]{0:T(128)S(6)} %copy.15.cut_ref, f32[2,4,512]{2,1,0:T(4,128)} %dir_ref.3), custom_call_target="tpu_custom_call" | custom-call | flops 100000000 | bytes 1000000 | tf_op jit(solution)/shard_map/pallas_call | solution.py:293
  3.4 17.1 %all-to-all-start = ((f32[64,1,384]{2,1,0:T(1,128)}), f32[64,1,384]{2,1,0:T(1,128)S(1)}, u32[]{:S(2)}, u32[]{:S(2)}) async-start(f32[64,1,384]{2,1,0:T(1,128)} %get-tuple-element.10), calls=%async_computation | async-start | bytes 196608 | tf_op jit(solution)/shard_map/all_to_all | solution.py:338
  21.2 0.0 copy-start
  21.2 0.7 copy-done
  21.9 0.0 copy-start.5
  21.9 1.1 %copy-done.5 = bf16[2,2,48,1536]{3,2,1,0:T(8,128)(2,1)S(1)} copy-done((bf16[2,2,48,1536]{3,2,1,0:T(8,128)(2,1)S(1)}, bf16[2,2,48,1536]{3,2,1,0:T(8,128)(2,1)}, u32[]{:S(2)}) %copy-start.5) | copy-done | bytes 589848
  22.9 0.0 copy-start.6
  22.9 0.7 copy-done.6
  23.6 0.0 copy-start.1
  23.6 3.9 %shard_map.122 = (bf16[2,256,2048]{2,1,0:T(8,128)(2,1)S(1)}, f32[2,2048]{1,0:T(2,128)S(1)}, f32[1,2048]{1,0:T(1,128)S(1)}) custom-call(s32[1]{0:T(128)S(6)} %copy.14.count_ref, s32[1,2048]{1,0:T(1,128)S(1)} %copy-done, f32[1,2048]{1,0:T(1,128)S(1)} %copy-done.6, bf16[192,1536]{1,0:T(8,128)(2,1)S(1)} %bitcast.5), custom_call_target="tpu_custom_call" | custom-call | flops 2000000000 | bytes 4000000 | tf_op jit(solution)/shard_map/pallas_call | solution.py:303
  27.5 3.8 %all-to-all-done.recv_ref = f32[64,1,384]{2,1,0:T(1,128)S(1)} async-done(((f32[64,1,384]{2,1,0:T(1,128)}), f32[64,1,384]{2,1,0:T(1,128)S(1)}, u32[]{:S(2)}, u32[]{:S(2)}) %all-to-all-start) | async-done | bytes 98336 | tf_op jit(solution)/shard_map/all_to_all | solution.py:338
  31.3 0.0 copy-done.1
  31.3 0.0 copy-start.2
  31.3 0.0 copy-start.3
  31.3 0.0 copy-start.7
  31.3 0.0 copy-start.8
  31.3 0.0 copy-start.9
  31.3 0.7 shard_map.123
  32.0 0.0 copy-start.4
  32.0 11.1 %all_to_all.25.parts_ref = f32[8,16,128]{2,1,0:T(8,128)S(1)} all-to-all(f32[8,16,128]{2,1,0:T(8,128)S(1)} %broadcast_in_dim.8), channel_id=1, replica_groups=mesh['mem'=8,'sp'=64] {'mem'}, dimensions={0} | all-to-all | bytes 131072 | tf_op jit(solution)/shard_map/all_to_all | solution.py:343
  43.1 0.8 shard_map.124
  43.9 17.9 %all_to_all.26.recv_ref = f32[64,1,384]{2,1,0:T(1,128)S(1)} all-to-all(f32[64,1,384]{2,1,0:T(1,128)S(1)} %shard_map.124), channel_id=1, replica_groups={{0,63,45,18,44,19,1,62,37,26,8,55,9,54,36,27,16,47,61,2,60,3,17,46,53,1..., dimensions={0} | all-to-all | bytes 196608 | tf_op jit(solution)/shard_map/all_to_all | solution.py:338
  61.9 0.0 copy-done.2
  61.9 0.0 copy-done.3
  61.9 0.0 copy-done.7
  61.9 0.0 copy-done.8
  61.9 0.0 copy-done.9
  61.9 0.9 shard_map.125
  62.8 10.7 %all_to_all.27 = f32[16,1,128]{2,1,0:T(1,128)S(1)} all-to-all(f32[16,1,128]{2,1,0:T(1,128)S(1)} %broadcast_in_dim.10), channel_id=1, replica_groups={{0,449,385,64,192,257,321,128,1,448,384,65,193,256,320,129},{2,451,387,..., dimensions={0} | all-to-all | bytes 16384 | tf_op jit(solution)/shard_map/all_to_all | solution.py:343
  73.5 13.9 %all_to_all.28.parts_ref = f32[32,1,128]{2,1,0:T(1,128)S(1)} all-to-all(f32[32,1,128]{2,1,0:T(1,128)S(1)} %broadcast_in_dim.11), channel_id=1, replica_groups={{0,62,46,16,52,10,26,36,54,8,24,38,2,60,44,18,6,56,40,22,50,12,28,34,48..., dimensions={0} | all-to-all | bytes 32768 | tf_op jit(solution)/shard_map/all_to_all | solution.py:343
  87.4 0.0 copy-done.4
  87.4 0.7 shard_map.126
  (4 shorter events, 0.0 us)
Async XLA Ops:
  3.4 27.9 %all-to-all-start = ((f32[64,1,384]{2,1,0:T(1,128)}), f32[64,1,384]{2,1,0:T(1,128)S(1)}, u32[]{:S(2)}, u32[]{:S(2)}) async-start(f32[64,1,384]{2,1,0:T(1,128)} %get-tuple-element.10), calls=%async_computation | async-start | bytes 196608 | tf_op jit(solution)/shard_map/all_to_all | solution.py:338
  21.2 0.7 copy-start
  21.9 1.1 %copy-start.5 = (bf16[2,2,48,1536]{3,2,1,0:T(8,128)(2,1)S(1)}, bf16[2,2,48,1536]{3,2,1,0:T(8,128)(2,1)}, u32[]{:S(2)}) copy-start(bf16[2,2,48,1536]{3,2,1,0:T(8,128)(2,1)} %param.13) | copy-start | bytes 1769476
  22.9 0.7 copy-start.6
  23.6 7.7 %copy-start.1 = (s32[1,2048]{1,0:T(1,128)S(1)}, s32[1,2048]{1,0:T(1,128)}, u32[]{:S(2)}) copy-start(s32[1,2048]{1,0:T(1,128)} %index_ref.5) | copy-start | bytes 24580
  31.3 30.6 %copy-start.2 = (f32[2,4,512]{2,1,0:T(4,128)S(1)}, f32[2,4,512]{2,1,0:T(4,128)}, u32[]{:S(2)}) copy-start(f32[2,4,512]{2,1,0:T(4,128)} %dir_ref.3) | copy-start | bytes 49156
  31.3 30.6 %copy-start.3 = (f32[2,4,512]{2,1,0:T(4,128)S(1)}, f32[2,4,512]{2,1,0:T(4,128)}, u32[]{:S(2)}) copy-start(f32[2,4,512]{2,1,0:T(4,128)} %grad_ref.3) | copy-start | bytes 49156
  31.3 30.6 %copy-start.7 = (f32[2,64,256]{2,1,0:T(8,128)S(1)}, f32[2,64,256]{2,1,0:T(8,128)}, u32[]{:S(2)}) copy-start(f32[2,64,256]{2,1,0:T(8,128)} %constant.10.clone.phase_ref) | copy-start | bytes 393220
  31.3 30.6 %copy-start.8 = (f32[48,512]{1,0:T(8,128)S(1)}, f32[48,512]{1,0:T(8,128)}, u32[]{:S(2)}) copy-start(f32[48,512]{1,0:T(8,128)} %constant.11.clone.rows_ref) | copy-start | bytes 294916
  31.3 30.6 %copy-start.9 = (f32[4,512]{1,0:T(4,128)S(1)}, f32[4,512]{1,0:T(4,128)}, u32[]{:S(2)}) copy-start(f32[4,512]{1,0:T(4,128)} %get-tuple-element.14.amp_ref) | copy-start | bytes 24580
  32.0 55.4 %copy-start.4 = (f32[2,4,512]{2,1,0:T(4,128)S(1)}, f32[2,4,512]{2,1,0:T(4,128)}, u32[]{:S(2)}) copy-start(f32[2,4,512]{2,1,0:T(4,128)} %cont_ref.1) | copy-start | bytes 49156

commit v5 on v3

--- a/solution.py
+++ b/solution.py
@@ -125,10 +125,8 @@
     return (product - jnp.floor(product * (1.0 / length)) * length) * (1.0 / length)
 
 
-def at_slots(count_ref, index_ref, weight_ref, pert_ref, basis_ref, values_ref, masked_ref):
+def at_slots(index_ref, pert_ref, basis_ref, values_ref):
     block = 256
-    usable = lax.broadcasted_iota(i32, (1, SLOTS), 1) < count_ref[0]
-    masked_ref[...] = jnp.where(usable, weight_ref[...] * (SCALE * SCALE), 0.0)
 
     @pl.loop(0, SLOTS // block)
     def _(step):
@@ -176,10 +174,11 @@
     out_ref[...] = jnp.concatenate([total[:, i * 128:(i + 1) * 128] for i in range(SLOTS // 128)], axis=0)
 
 
-def spread(parts_ref, masked_ref, basis_ref, values_ref, index_ref, out_ref):
+def spread(count_ref, parts_ref, weight_ref, basis_ref, values_ref, index_ref, out_ref):
     sampled = jnp.sum(parts_ref[...], axis=0)
     sampled = jnp.concatenate([sampled[i:i + 1] for i in range(SLOTS // 128)], axis=1)
-    weighted = masked_ref[...] * sampled
+    usable = lax.broadcasted_iota(i32, (1, SLOTS), 1) < count_ref[0]
+    weighted = jnp.where(usable, (weight_ref[...] * (SCALE * SCALE)) * sampled, 0.0)
     line, _ = cell_parts(index_ref)
     row = jnp.where(line >= ROWS, line - ROWS, line)
     mine = lax.broadcasted_iota(i32, (ROWS, SLOTS), 0) == row
@@ -277,12 +276,12 @@
     )(pencil, cutoff, direction)
 
 
-def stage_at_slots(count, index, weight, perturb):
-    return call(
-        at_slots, [SMEM] + [VMEM] * 3,
-        [((2, 2 * KB, SLOTS), bf16), ((LOCAL_M, SLOTS), f32), ((1, SLOTS), f32)],
+def stage_at_slots(index, perturb):
+    return call(
+        at_slots, [VMEM] * 2,
+        [((2, 2 * KB, SLOTS), bf16), ((LOCAL_M, SLOTS), f32)],
         flops=2 * 10 ** 9, moved=4 * 10 ** 6,
-    )(count, index, weight, perturb)
+    )(index, perturb)
 
 
 def stage_sample(recv, basis, values, index):
@@ -291,10 +290,10 @@
     )(recv, basis, values, index)[0]
 
 
-def stage_spread(parts, masked, basis, values, index):
-    return call(
-        spread, [VMEM] * 5, [((N_SP, 1, CHUNK), f32)], flops=3 * 10 ** 8, moved=2 * 10 ** 6,
-    )(parts, masked, basis, values, index)[0]
+def stage_spread(count, parts, weight, basis, values, index):
+    return call(
+        spread, [SMEM] + [VMEM] * 5, [((N_SP, 1, CHUNK), f32)], flops=3 * 10 ** 8, moved=2 * 10 ** 6,
+    )(count, parts, weight, basis, values, index)[0]
 
 
 def stage_from_rows(recv, phase, rows, amp, direction, gradient):
@@ -328,10 +327,9 @@
 def shards(phase, rows, control, gradient, direction, perturb, obs_index, obs_count, obs_weight, cutoff):
     pencil = lax.axis_index("sp").astype(i32).reshape(1)
     send, amp = stage_to_rows(pencil, cutoff, direction)
-    basis, values, masked = stage_at_slots(
-        obs_count, obs_index, obs_weight, perturb.reshape(LOCAL_M * LEVELS * ROWS, NB))
+    basis, values = stage_at_slots(obs_index, perturb.reshape(LOCAL_M * LEVELS * ROWS, NB))
     part = stage_sample(swap(send), basis, values, obs_index)
-    send = stage_spread(share(part, "mem", SIDE), masked, basis, values, obs_index)
+    send = stage_spread(obs_count, share(part, "mem", SIDE), obs_weight, basis, values, obs_index)
     product, sums = stage_from_rows(swap(send), phase, rows, amp, direction, gradient)
     sums = jnp.sum(share(sums, ("mem", "sp"), len(NEAR[0]), NEAR), axis=0)
     sums = share(sums, ("mem", "sp"), len(FAR[0]), FAR)

time: 88.9 us -> 88.3 us (level)
  blocking collectives: 53.2 us -> 40.9 us
  starting transfers between devices: 17.1 us -> 23.5 us
  waiting for transfers between devices: 4.42 us -> 9.97 us
    all_to_all x3 -> x2, blocking collectives: 35.1 us -> 24.1 us  [share(): return lax.all_to_all(x, axis, 0, 0, axis_index_groups=groups, tiled=True)]
    all_to_all x0 -> x1, starting transfers between devices: none -> 6.31 us  [share(): return lax.all_to_all(x, axis, 0, 0, axis_index_groups=groups, tiled=True)]
    all_to_all x0 -> x1, waiting for transfers between devices: none -> 4.2 us  [share(): return lax.all_to_all(x, axis, 0, 0, axis_index_groups=groups, tiled=True)]
    all_to_all x1, blocking collectives: 18.1 us -> 16.7 us  [swap(): return lax.all_to_all(x, 'sp', 0, 0, tiled=True)]
    all_to_all x1, waiting for transfers between devices: 4.42 us -> 5.77 us  [swap(): return lax.all_to_all(x, 'sp', 0, 0, tiled=True)]
  transfers between devices with their start and end apart: 1 -> 2, of which waited for: 1 -> 2; matrix products, arithmetic and copies ran while one was open for 0% -> 0% of each run, Pallas kernels for 4% -> 4%
where the time goes in v5:
time: 88.3 us; the launch traced here: 87.8 us
  blocking collectives  40.9 us (46%)
  starting transfers between devices  23.5 us (27%)
  waiting for transfers between devices  9.97 us (11%)
  Pallas kernels  9.04 us (10%)
  local copies, waits for them, and re-layouts  2.44 us (3%)
  between operations  2.04 us (2%)
    all_to_all x2, blocking collectives, share(): return lax.all_to_all(x, axis, 0, 0, axis_index_groups=groups, tiled=True)  24.1 us
    all_to_all x1, starting transfers between devices, swap(): return lax.all_to_all(x, 'sp', 0, 0, tiled=True)  17.1 us
    all_to_all x1, blocking collectives, swap(): return lax.all_to_all(x, 'sp', 0, 0, tiled=True)  16.7 us
    all_to_all x1, starting transfers between devices, share(): return lax.all_to_all(x, axis, 0, 0, axis_index_groups=groups, tiled=True)  6.31 us
    all_to_all x1, waiting for transfers between devices, swap(): return lax.all_to_all(x, 'sp', 0, 0, tiled=True)  5.77 us
    all_to_all x1, waiting for transfers between devices, share(): return lax.all_to_all(x, axis, 0, 0, axis_index_groups=groups, tiled=True)  4.2 us
    pallas_call x1, Pallas kernels, stage_at_slots(): call(at_slots, [VMEM] * 2, [((2, 2 * KB, SLOTS), bf16), ((LOCAL_M, SLOTS)...  3.83 us
    pallas_call x1, Pallas kernels, stage_to_rows(): call(to_rows, [SMEM, SMEM, HBM], [((N_SP, 1, CHUNK), f32), ((LOCAL_KB, 2...  2.07 us
  transfers between devices with their start and end apart: 2, of which 2 were waited for; matrix products, arithmetic and copies ran while one was open for 0% of the time, Pallas kernels for 4%

profile of v5, /device:TPU:1, one launch (start us, length us, event | category | flops | bytes accessed | tf_op | source)
XLA Modules:
  0.0 87.8 jit_solution(2429021670644243534)
XLA Ops:
  1.3 2.1 %shard_map.121 = (f32[64,1,384]{2,1,0:T(1,128)}, f32[4,512]{1,0:T(4,128)}) custom-call(s32[1]{0:T(128)} %bitcast.pen_ref, s32[1]{0:T(128)S(6)} %copy.15.cut_ref, f32[2,4,512]{2,1,0:T(4,128)} %dir_ref.3), custom_call_target="tpu_custom_call" | custom-call | flops 100000000 | bytes 1000000 | tf_op jit(solution)/shard_map/pallas_call | solution.py:270
  3.4 17.1 %all-to-all-start = ((f32[64,1,384]{2,1,0:T(1,128)}), f32[64,1,384]{2,1,0:T(1,128)S(1)}, u32[]{:S(2)}, u32[]{:S(2)}) async-start(f32[64,1,384]{2,1,0:T(1,128)} %get-tuple-element.9), calls=%async_computation | async-start | bytes 196608 | tf_op jit(solution)/shard_map/all_to_all | solution.py:319
  20.5 0.0 copy-start
  20.5 0.7 copy-done
  21.2 0.0 copy-start.6
  21.2 1.1 %copy-done.6 = bf16[2,2,48,1536]{3,2,1,0:T(8,128)(2,1)S(1)} copy-done((bf16[2,2,48,1536]{3,2,1,0:T(8,128)(2,1)S(1)}, bf16[2,2,48,1536]{3,2,1,0:T(8,128)(2,1)}, u32[]{:S(2)}) %copy-start.6) | copy-done | bytes 589848
  22.3 0.0 copy-start.1
  22.3 3.8 %shard_map.122 = (bf16[2,256,2048]{2,1,0:T(8,128)(2,1)S(1)}, f32[2,2048]{1,0:T(2,128)S(1)}) custom-call(s32[1,2048]{1,0:T(1,128)S(1)} %copy-done, bf16[192,1536]{1,0:T(8,128)(2,1)S(1)} %bitcast.5), custom_call_target="tpu_custom_call" | custom-call | flops 2000000000 | bytes 4000000 | tf_op jit(solution)/shard_map/pallas_call | solution.py:280
  26.1 0.0 copy-start.5
  26.1 5.8 %all-to-all-done.recv_ref = f32[64,1,384]{2,1,0:T(1,128)S(1)} async-done(((f32[64,1,384]{2,1,0:T(1,128)}), f32[64,1,384]{2,1,0:T(1,128)S(1)}, u32[]{:S(2)}, u32[]{:S(2)}) %all-to-all-start) | async-done | bytes 98336 | tf_op jit(solution)/shard_map/all_to_all | solution.py:319
  31.9 0.0 copy-done.1
  31.9 0.0 copy-start.2
  31.9 0.0 copy-start.3
  31.9 0.0 copy-start.7
  31.9 0.0 copy-start.8
  31.9 0.0 copy-start.9
  31.9 0.7 shard_map.123
  32.6 0.0 copy-start.4
  32.6 0.6 broadcast_in_dim.8
  33.3 6.3 %all-to-all-start.1 = ((f32[8,16,128]{2,1,0:T(8,128)}), f32[8,16,128]{2,1,0:T(8,128)S(1)}, u32[]{:S(2)}, u32[]{:S(2)}) async-start(f32[8,16,128]{2,1,0:T(8,128)} %broadcast_in_dim.8), calls=%async_computation.1 | async-start | bytes 131072 | tf_op jit(solution)/shard_map/all_to_all | solution.py:324
  40.2 4.2 %all-to-all-done.1.parts_ref = f32[8,16,128]{2,1,0:T(8,128)S(1)} async-done(((f32[8,16,128]{2,1,0:T(8,128)}), f32[8,16,128]{2,1,0:T(8,128)S(1)}, u32[]{:S(2)}, u32[]{:S(2)}) %all-to-all-start.1) | async-done | bytes 65568 | tf_op jit(solution)/shard_map/all_to_all | solution.py:324
  44.4 0.0 copy-done.5
  44.4 0.8 shard_map.124
  45.3 16.7 %all_to_all.25.recv_ref = f32[64,1,384]{2,1,0:T(1,128)S(1)} all-to-all(f32[64,1,384]{2,1,0:T(1,128)S(1)} %shard_map.124), channel_id=1, replica_groups=mesh['mem'=8,'sp'=64] {'sp'}, dimensions={0} | all-to-all | bytes 196608 | tf_op jit(solution)/shard_map/all_to_all | solution.py:319
  62.0 0.0 copy-done.2
  62.0 0.0 copy-done.3
  62.0 0.0 copy-done.7
  62.0 0.0 copy-done.8
  62.0 0.0 copy-done.9
  62.0 0.9 shard_map.125
  62.9 10.2 %all_to_all.26 = f32[16,1,128]{2,1,0:T(1,128)S(1)} all-to-all(f32[16,1,128]{2,1,0:T(1,128)S(1)} %broadcast_in_dim.10), channel_id=1, replica_groups={{0,1,64,65,128,129,192,193,256,257,320,321,384,385,448,449},{2,3,66,67,..., dimensions={0} | all-to-all | bytes 16384 | tf_op jit(solution)/shard_map/all_to_all | solution.py:324
  73.1 14.0 %all_to_all.27.parts_ref = f32[32,1,128]{2,1,0:T(1,128)S(1)} all-to-all(f32[32,1,128]{2,1,0:T(1,128)S(1)} %broadcast_in_dim.11), channel_id=1, replica_groups={{0,2,4,6,8,10,12,14,16,18,20,22,24,26,28,30,32,34,36,38,40,42,44,46,48,..., dimensions={0} | all-to-all | bytes 32768 | tf_op jit(solution)/shard_map/all_to_all | solution.py:324
  87.1 0.0 copy-done.4
  87.1 0.7 shard_map.126
  (3 shorter events, 0.0 us)
Async XLA Ops:
  3.4 28.5 %all-to-all-start = ((f32[64,1,384]{2,1,0:T(1,128)}), f32[64,1,384]{2,1,0:T(1,128)S(1)}, u32[]{:S(2)}, u32[]{:S(2)}) async-start(f32[64,1,384]{2,1,0:T(1,128)} %get-tuple-element.9), calls=%async_computation | async-start | bytes 196608 | tf_op jit(solution)/shard_map/all_to_all | solution.py:319
  20.5 0.7 copy-start
  21.2 1.1 %copy-start.6 = (bf16[2,2,48,1536]{3,2,1,0:T(8,128)(2,1)S(1)}, bf16[2,2,48,1536]{3,2,1,0:T(8,128)(2,1)}, u32[]{:S(2)}) copy-start(bf16[2,2,48,1536]{3,2,1,0:T(8,128)(2,1)} %param.13) | copy-start | bytes 1769476
  22.3 9.6 %copy-start.1 = (s32[1,2048]{1,0:T(1,128)S(1)}, s32[1,2048]{1,0:T(1,128)}, u32[]{:S(2)}) copy-start(s32[1,2048]{1,0:T(1,128)} %index_ref.5) | copy-start | bytes 24580
  26.1 18.3 %copy-start.5 = (f32[1,2048]{1,0:T(1,128)S(1)}, f32[1,2048]{1,0:T(1,128)}, u32[]{:S(2)}) copy-start(f32[1,2048]{1,0:T(1,128)} %weight_ref.1) | copy-start | bytes 24580
  31.9 30.1 %copy-start.2 = (f32[2,4,512]{2,1,0:T(4,128)S(1)}, f32[2,4,512]{2,1,0:T(4,128)}, u32[]{:S(2)}) copy-start(f32[2,4,512]{2,1,0:T(4,128)} %dir_ref.3) | copy-start | bytes 49156
  31.9 30.1 %copy-start.3 = (f32[2,4,512]{2,1,0:T(4,128)S(1)}, f32[2,4,512]{2,1,0:T(4,128)}, u32[]{:S(2)}) copy-start(f32[2,4,512]{2,1,0:T(4,128)} %grad_ref.3) | copy-start | bytes 49156
  31.9 30.1 %copy-start.7 = (f32[2,64,256]{2,1,0:T(8,128)S(1)}, f32[2,64,256]{2,1,0:T(8,128)}, u32[]{:S(2)}) copy-start(f32[2,64,256]{2,1,0:T(8,128)} %constant.10.clone.phase_ref) | copy-start | bytes 393220
  31.9 30.1 %copy-start.8 = (f32[48,512]{1,0:T(8,128)S(1)}, f32[48,512]{1,0:T(8,128)}, u32[]{:S(2)}) copy-start(f32[48,512]{1,0:T(8,128)} %constant.11.clone.rows_ref) | copy-start | bytes 294916
  31.9 30.1 %copy-start.9 = (f32[4,512]{1,0:T(4,128)S(1)}, f32[4,512]{1,0:T(4,128)}, u32[]{:S(2)}) copy-start(f32[4,512]{1,0:T(4,128)} %get-tuple-element.12.amp_ref) | copy-start | bytes 24580
  32.6 54.4 %copy-start.4 = (f32[2,4,512]{2,1,0:T(4,128)S(1)}, f32[2,4,512]{2,1,0:T(4,128)}, u32[]{:S(2)}) copy-start(f32[2,4,512]{2,1,0:T(4,128)} %cont_ref.1) | copy-start | bytes 49156
  33.3 11.2 %all-to-all-start.1 = ((f32[8,16,128]{2,1,0:T(8,128)}), f32[8,16,128]{2,1,0:T(8,128)S(1)}, u32[]{:S(2)}, u32[]{:S(2)}) async-start(f32[8,16,128]{2,1,0:T(8,128)} %broadcast_in_dim.8), calls=%async_computation.1 | async-start | bytes 131072 | tf_op jit(solution)/shard_map/all_to_all | solution.py:324

commit v6 on v5

--- a/solution.py
+++ b/solution.py
@@ -59,14 +59,16 @@
 def to_rows(pen_ref, cut_ref, dir_in, out_ref, amp_ref, high_ref, low_ref, dir_ref, sem):
     dir_copy = pltpu.make_async_copy(dir_in, dir_ref, sem)
     dir_copy.start()
-    w = lax.broadcasted_iota(i32, (1, KA), 1)
+    w = lax.broadcasted_iota(i32, (1, 128), 1)
     s = lax.broadcasted_iota(i32, (N_SP, 1), 0)
     phase_c, phase_s = turns_to_cos_sin(((s * w) & (N_SP - 1)).astype(f32) * (1.0 / N_SP))
+    phase_c = jnp.concatenate([phase_c, phase_c], axis=1)
+    phase_s = jnp.concatenate([phase_s, phase_s], axis=1)
     r = lax.broadcasted_iota(i32, (ROWS, 1), 0)
-    slot = lax.broadcasted_iota(i32, (1, 2 * KA), 1)
-    ws = jnp.where(slot < KA, slot, jnp.where(slot == KA, KA, slot - KA))
+    w = lax.broadcasted_iota(i32, (1, KA), 1)
+    ws = jnp.where(w == 0, KA, w)
     cos_r, sin_r = turns_to_cos_sin(residue_turns(ws.astype(f32), r.astype(f32), NA))
-    table_high, table_low = split(jnp.where(slot < KA, cos_r, sin_r))
+    table_high, table_low = split(jnp.concatenate([jnp.where(w == 0, 1.0, cos_r), sin_r], axis=1))
     cutoff, pencil = cut_ref[0], pen_ref[0]
     wa = lax.broadcasted_iota(i32, (1, 384), 1)
     wb = lax.broadcasted_iota(i32, (136, 1), 0)
@@ -171,7 +173,9 @@
     for m in range(LOCAL_M):
         part = jnp.sum(jnp.where(mine, rows[m * ROWS:(m + 1) * ROWS], 0.0), axis=0, keepdims=True)
         total += values_ref[m:m + 1] * part
-    out_ref[...] = jnp.concatenate([total[:, i * 128:(i + 1) * 128] for i in range(SLOTS // 128)], axis=0)
+    dense = jnp.concatenate([total[:, i * 128:(i + 1) * 128] for i in range(SLOTS // 128)], axis=0)
+    for i in range(SIDE):
+        out_ref[i] = dense
 
 
 def spread(count_ref, parts_ref, weight_ref, basis_ref, values_ref, index_ref, out_ref):
@@ -203,7 +207,7 @@
     return x[:, :128] + x[:, 128:256] + x[:, 256:384] + x[:, 384:]
 
 
-def from_rows(recv_ref, phase_ref, rows_ref, amp_ref, dir_ref, grad_ref, prod_ref, sums_ref):
+def from_rows(recv_ref, phase_ref, rows_ref, amp_ref, dir_ref, grad_ref, square_ref, prod_ref, sums_ref):
     count = LOCAL_M * LOCAL_KB
     recv = recv_ref[:, 0, :]
     left = jnp.concatenate([recv[:, i * ROWS:(i + 1) * ROWS] for i in range(count)], axis=0)
@@ -213,7 +217,7 @@
     turned = dot(high, table_high, nn) + dot(high, table_low, nn) + dot(low, table_high, nn)
     phase_c, phase_s = phase_ref[0], phase_ref[1]
     amp = amp_ref[...]
-    totals = [jnp.zeros((1, 128), f32)] * 4
+    totals = [jnp.zeros((1, 128), f32)] * 3
     for m in range(LOCAL_M):
         part_c, part_s = [], []
         for k in range(LOCAL_KB):
@@ -226,11 +230,11 @@
         d, g = dir_ref[m], grad_ref[m]
         product = d + amp * jnp.concatenate([back_c, back_s], axis=1)
         prod_ref[m] = product
-        terms = (g * g, d * product, g * product, product * product)
+        terms = (d * product, g * product, product * product)
         totals = [t + fold(x) for t, x in zip(totals, terms)]
     lane = lax.broadcasted_iota(i32, (1, 128), 1)
     line = jnp.zeros((1, 128), f32)
-    for k, t in enumerate(totals):
+    for k, t in enumerate([fold(square_ref[...])] + totals):
         t = t + pltpu.roll(t, 64, 1)
         t = t + pltpu.roll(t, 32, 1)
         line = jnp.where((lane >> 5) == k, t, line)
@@ -286,7 +290,7 @@
 
 def stage_sample(recv, basis, values, index):
     return call(
-        sample, [VMEM] * 4, [((SLOTS // 128, 128), f32)], flops=3 * 10 ** 8, moved=2 * 10 ** 6,
+        sample, [VMEM] * 4, [((SIDE, SLOTS // 128, 128), f32)], flops=3 * 10 ** 8, moved=2 * 10 ** 6,
     )(recv, basis, values, index)[0]
 
 
@@ -296,12 +300,12 @@
     )(count, parts, weight, basis, values, index)[0]
 
 
-def stage_from_rows(recv, phase, rows, amp, direction, gradient):
-    return call(
-        from_rows, [VMEM] * 6,
+def stage_from_rows(recv, phase, rows, amp, direction, gradient, square):
+    return call(
+        from_rows, [VMEM] * 7,
         [((LOCAL_M, LOCAL_KB, 2 * KA), f32), ((1, 128), f32)],
         flops=10 ** 8, moved=10 ** 6,
-    )(recv, phase, rows, amp, direction, gradient)
+    )(recv, phase, rows, amp, direction, gradient, square)
 
 
 def stage_update(parts, control, gradient, direction, product):
@@ -328,9 +332,10 @@
     pencil = lax.axis_index("sp").astype(i32).reshape(1)
     send, amp = stage_to_rows(pencil, cutoff, direction)
     basis, values = stage_at_slots(obs_index, perturb.reshape(LOCAL_M * LEVELS * ROWS, NB))
-    part = stage_sample(swap(send), basis, values, obs_index)
-    send = stage_spread(obs_count, share(part, "mem", SIDE), obs_weight, basis, values, obs_index)
-    product, sums = stage_from_rows(swap(send), phase, rows, amp, direction, gradient)
+    parts = lax.all_to_all(stage_sample(swap(send), basis, values, obs_index), "mem", 0, 0, tiled=True)
+    send = stage_spread(obs_count, parts, obs_weight, basis, values, obs_index)
+    square = jnp.sum(gradient * gradient, axis=(0, 1))[None]
+    product, sums = stage_from_rows(swap(send), phase, rows, amp, direction, gradient, square)
     sums = jnp.sum(share(sums, ("mem", "sp"), len(NEAR[0]), NEAR), axis=0)
     sums = share(sums, ("mem", "sp"), len(FAR[0]), FAR)
     return tuple(stage_update(sums, control, gradient, direction, product))

time: 88.3 us -> 89.3 us (1.011)
  blocking collectives: 40.9 us -> 24.1 us
  waiting for transfers between devices: 9.97 us -> 21.2 us
  starting transfers between devices: 23.5 us -> 29.2 us
  Pallas kernels: 9.04 us -> 10.3 us
    all_to_all x1 -> x0, blocking collectives: 16.7 us -> none  [swap(): return lax.all_to_all(x, 'sp', 0, 0, tiled=True)]
    all_to_all x1 -> x2, waiting for transfers between devices: 5.77 us -> 17 us  [swap(): return lax.all_to_all(x, 'sp', 0, 0, tiled=True)]
    all_to_all x1 -> x2, starting transfers between devices: 17.1 us -> 22.8 us  [swap(): return lax.all_to_all(x, 'sp', 0, 0, tiled=True)]
  transfers between devices with their start and end apart: 2 -> 3, of which waited for: 2 -> 3; matrix products, arithmetic and copies ran while one was open for 0% -> 0% of each run, Pallas kernels for 4% -> 4%
where the time goes in v6:
time: 89.3 us; the launch traced here: 88.7 us
  starting transfers between devices  29.2 us (33%)
  blocking collectives  24.1 us (27%)
  waiting for transfers between devices  21.2 us (24%)
  Pallas kernels  10.3 us (12%)
  between operations  2.03 us (2%)
  local copies, waits for them, and re-layouts  1.82 us (2%)
    all_to_all x2, blocking collectives, share(): return lax.all_to_all(x, axis, 0, 0, axis_index_groups=groups, tiled=True)  24.1 us
    all_to_all x2, starting transfers between devices, swap(): return lax.all_to_all(x, 'sp', 0, 0, tiled=True)  22.8 us
    all_to_all x2, waiting for transfers between devices, swap(): return lax.all_to_all(x, 'sp', 0, 0, tiled=True)  17 us
    all_to_all x1, starting transfers between devices, shards(): lax.all_to_all(stage_sample(swap(send), basis, values, obs_index), 'mem',...  6.44 us
    all_to_all x1, waiting for transfers between devices, shards(): lax.all_to_all(stage_sample(swap(send), basis, values, obs_index), 'mem',...  4.2 us
    pallas_call x1, Pallas kernels, stage_at_slots(): call(at_slots, [VMEM] * 2, [((2, 2 * KB, SLOTS), bf16), ((LOCAL_M, SLOTS)...  3.84 us
    pallas_call x1, Pallas kernels, stage_to_rows(): call(to_rows, [SMEM, SMEM, HBM], [((N_SP, 1, CHUNK), f32), ((LOCAL_KB, 2...  2.06 us
    unnamed x20, local copies, waits for them, and re-layouts  1.79 us
  transfers between devices with their start and end apart: 3, of which 3 were waited for; matrix products, arithmetic and copies ran while one was open for 0% of the time, Pallas kernels for 4%

profile of v6, /device:TPU:1, one launch (start us, length us, event | category | flops | bytes accessed | tf_op | source)
XLA Modules:
  0.0 88.7 jit_solution(2641933650756798597)
XLA Ops:
  1.3 2.1 %shard_map.121 = (f32[64,1,384]{2,1,0:T(1,128)}, f32[4,512]{1,0:T(4,128)}) custom-call(s32[1]{0:T(128)} %bitcast.pen_ref, s32[1]{0:T(128)S(6)} %copy.15.cut_ref, f32[2,4,512]{2,1,0:T(4,128)} %dir_ref.3), custom_call_target="tpu_custom_call" | custom-call | flops 100000000 | bytes 1000000 | tf_op jit(solution)/shard_map/pallas_call | solution.py:274
  3.3 17.1 %all-to-all-start = ((f32[64,1,384]{2,1,0:T(1,128)}), f32[64,1,384]{2,1,0:T(1,128)S(1)}, u32[]{:S(2)}, u32[]{:S(2)}) async-start(f32[64,1,384]{2,1,0:T(1,128)} %get-tuple-element.9), calls=%async_computation | async-start | bytes 196608 | tf_op jit(solution)/shard_map/all_to_all | solution.py:323
  20.5 0.0 copy-start.4
  20.5 0.7 copy-done.4
  21.2 0.0 copy-start.9
  21.2 1.1 %copy-done.9 = bf16[2,2,48,1536]{3,2,1,0:T(8,128)(2,1)S(1)} copy-done((bf16[2,2,48,1536]{3,2,1,0:T(8,128)(2,1)S(1)}, bf16[2,2,48,1536]{3,2,1,0:T(8,128)(2,1)}, u32[]{:S(2)}) %copy-start.9) | copy-done | bytes 589848
  22.3 0.0 copy-start.5
  22.3 3.8 %shard_map.122 = (bf16[2,256,2048]{2,1,0:T(8,128)(2,1)S(1)}, f32[2,2048]{1,0:T(2,128)S(1)}) custom-call(s32[1,2048]{1,0:T(1,128)S(1)} %copy-done.4, bf16[192,1536]{1,0:T(8,128)(2,1)S(1)} %bitcast.7), custom_call_target="tpu_custom_call" | custom-call | flops 2000000000 | bytes 4000000 | tf_op jit(solution)/shard_map/pallas_call | solution.py:284
  26.1 0.0 copy-start.7
  26.1 5.8 %all-to-all-done.recv_ref = f32[64,1,384]{2,1,0:T(1,128)S(1)} async-done(((f32[64,1,384]{2,1,0:T(1,128)}), f32[64,1,384]{2,1,0:T(1,128)S(1)}, u32[]{:S(2)}, u32[]{:S(2)}) %all-to-all-start) | async-done | bytes 98336 | tf_op jit(solution)/shard_map/all_to_all | solution.py:323
  31.9 0.0 copy-done.5
  31.9 0.0 copy-start
  31.9 0.0 copy-start.1
  31.9 0.0 copy-start.2
  31.9 0.0 copy-start.3
  31.9 0.0 copy-start.8
  31.9 1.3 %shard_map.123 = f32[8,16,128]{2,1,0:T(8,128)} custom-call(f32[64,1,384]{2,1,0:T(1,128)S(1)} %all-to-all-done.recv_ref, bf16[2,256,2048]{2,1,0:T(8,128)(2,1)S(1)} %get-tuple-element.10.basis_ref, f32[2,2048]{1,0:T(2,128)S(1)} %get-tuple-element.11.values_ref, s32[1,2048]{1,0:T(1,128)S(1)} %copy-done.5), custom_call_target="tpu_custom_call" | custom-call | flops 300000000 | bytes 2000000 | tf_op jit(solution)/shard_map/pallas_call | solution.py:292
  33.2 0.0 copy-start.6
  33.2 6.4 %all-to-all-start.1 = ((f32[8,16,128]{2,1,0:T(8,128)}), f32[8,16,128]{2,1,0:T(8,128)S(1)}, u32[]{:S(2)}, u32[]{:S(2)}) async-start(f32[8,16,128]{2,1,0:T(8,128)} %shard_map.123), calls=%async_computation.1 | async-start | bytes 131072 | tf_op jit(solution)/shard_map/all_to_all | solution.py:335
  40.3 4.2 %all-to-all-done.1.parts_ref = f32[8,16,128]{2,1,0:T(8,128)S(1)} async-done(((f32[8,16,128]{2,1,0:T(8,128)}), f32[8,16,128]{2,1,0:T(8,128)S(1)}, u32[]{:S(2)}, u32[]{:S(2)}) %all-to-all-start.1) | async-done | bytes 65568 | tf_op jit(solution)/shard_map/all_to_all | solution.py:335
  44.5 0.0 copy-done.7
  44.5 1.5 %shard_map.124 = f32[64,1,384]{2,1,0:T(1,128)} custom-call(s32[1]{0:T(128)S(6)} %copy.14.count_ref, f32[8,16,128]{2,1,0:T(8,128)S(1)} %all-to-all-done.1.parts_ref, f32[1,2048]{1,0:T(1,128)S(1)} %copy-done.7, bf16[2,256,2048]{2,1,0:T(8,128)(2,1)S(1)} %get-tuple-element.10.basis_ref, f32[2,2048]{1,0:T(2,128)S(1)} %get-tuple-element.11.values_ref, ...), custom_call_target="tpu_custom_call" | custom-call | flops 300000000 | bytes 2000000 | tf_op jit(solution)/shard_map/pallas_call | solution.py:298
  46.0 5.6 %all-to-all-start.2 = ((f32[64,1,384]{2,1,0:T(1,128)}), f32[64,1,384]{2,1,0:T(1,128)S(1)}, u32[]{:S(2)}, u32[]{:S(2)}) async-start(f32[64,1,384]{2,1,0:T(1,128)} %shard_map.124), calls=%async_computation.2 | async-start | bytes 196608 | tf_op jit(solution)/shard_map/all_to_all | solution.py:323
  51.6 0.0 copy-done
  51.7 11.3 %all-to-all-done.2.recv_ref = f32[64,1,384]{2,1,0:T(1,128)S(1)} async-done(((f32[64,1,384]{2,1,0:T(1,128)}), f32[64,1,384]{2,1,0:T(1,128)S(1)}, u32[]{:S(2)}, u32[]{:S(2)}) %all-to-all-start.2) | async-done | bytes 98336 | tf_op jit(solution)/shard_map/all_to_all | solution.py:323
  62.9 0.0 copy-done.1
  62.9 0.0 copy-done.2
  63.0 0.0 copy-done.3
  63.0 0.0 copy-done.8
  63.0 0.9 shard_map.125
  63.8 10.2 %all_to_all.25 = f32[16,1,128]{2,1,0:T(1,128)S(1)} all-to-all(f32[16,1,128]{2,1,0:T(1,128)S(1)} %broadcast_in_dim.19), channel_id=1, replica_groups={{0,1,64,65,128,129,192,193,256,257,320,321,384,385,448,449},{2,3,66,67,..., dimensions={0} | all-to-all | bytes 16384 | tf_op jit(solution)/shard_map/all_to_all | solution.py:328
  74.1 14.0 %all_to_all.26.parts_ref = f32[32,1,128]{2,1,0:T(1,128)S(1)} all-to-all(f32[32,1,128]{2,1,0:T(1,128)S(1)} %broadcast_in_dim.20), channel_id=1, replica_groups={{0,2,4,6,8,10,12,14,16,18,20,22,24,26,28,30,32,34,36,38,40,42,44,46,48,..., dimensions={0} | all-to-all | bytes 32768 | tf_op jit(solution)/shard_map/all_to_all | solution.py:328
  88.0 0.0 copy-done.6
  88.0 0.7 shard_map.126
  (4 shorter events, 0.1 us)
Async XLA Ops:
  3.3 28.5 %all-to-all-start = ((f32[64,1,384]{2,1,0:T(1,128)}), f32[64,1,384]{2,1,0:T(1,128)S(1)}, u32[]{:S(2)}, u32[]{:S(2)}) async-start(f32[64,1,384]{2,1,0:T(1,128)} %get-tuple-element.9), calls=%async_computation | async-start | bytes 196608 | tf_op jit(solution)/shard_map/all_to_all | solution.py:323
  20.5 0.7 copy-start.4
  21.2 1.1 %copy-start.9 = (bf16[2,2,48,1536]{3,2,1,0:T(8,128)(2,1)S(1)}, bf16[2,2,48,1536]{3,2,1,0:T(8,128)(2,1)}, u32[]{:S(2)}) copy-start(bf16[2,2,48,1536]{3,2,1,0:T(8,128)(2,1)} %param.13) | copy-start | bytes 1769476
  22.3 9.6 %copy-start.5 = (s32[1,2048]{1,0:T(1,128)S(1)}, s32[1,2048]{1,0:T(1,128)}, u32[]{:S(2)}) copy-start(s32[1,2048]{1,0:T(1,128)} %index_ref.5) | copy-start | bytes 24580
  26.1 18.4 %copy-start.7 = (f32[1,2048]{1,0:T(1,128)S(1)}, f32[1,2048]{1,0:T(1,128)}, u32[]{:S(2)}) copy-start(f32[1,2048]{1,0:T(1,128)} %weight_ref.1) | copy-start | bytes 24580
  31.9 19.7 %copy-start = (f32[2,4,512]{2,1,0:T(4,128)S(1)}, f32[2,4,512]{2,1,0:T(4,128)}, u32[]{:S(2)}) copy-start(f32[2,4,512]{2,1,0:T(4,128)} %grad_ref.3) | copy-start | bytes 49156
  31.9 31.0 %copy-start.1 = (f32[2,64,256]{2,1,0:T(8,128)S(1)}, f32[2,64,256]{2,1,0:T(8,128)}, u32[]{:S(2)}) copy-start(f32[2,64,256]{2,1,0:T(8,128)} %constant.10.clone.phase_ref) | copy-start | bytes 393220
  31.9 31.0 %copy-start.2 = (f32[48,512]{1,0:T(8,128)S(1)}, f32[48,512]{1,0:T(8,128)}, u32[]{:S(2)}) copy-start(f32[48,512]{1,0:T(8,128)} %constant.11.clone.rows_ref) | copy-start | bytes 294916
  31.9 31.0 %copy-start.3 = (f32[2,4,512]{2,1,0:T(4,128)S(1)}, f32[2,4,512]{2,1,0:T(4,128)}, u32[]{:S(2)}) copy-start(f32[2,4,512]{2,1,0:T(4,128)} %dir_ref.3) | copy-start | bytes 49156
  31.9 31.0 %copy-start.8 = (f32[4,512]{1,0:T(4,128)S(1)}, f32[4,512]{1,0:T(4,128)}, u32[]{:S(2)}) copy-start(f32[4,512]{1,0:T(4,128)} %get-tuple-element.12.amp_ref) | copy-start | bytes 24580
  33.2 54.8 %copy-start.6 = (f32[2,4,512]{2,1,0:T(4,128)S(1)}, f32[2,4,512]{2,1,0:T(4,128)}, u32[]{:S(2)}) copy-start(f32[2,4,512]{2,1,0:T(4,128)} %cont_ref.1) | copy-start | bytes 49156
  33.2 11.3 %all-to-all-start.1 = ((f32[8,16,128]{2,1,0:T(8,128)}), f32[8,16,128]{2,1,0:T(8,128)S(1)}, u32[]{:S(2)}, u32[]{:S(2)}) async-start(f32[8,16,128]{2,1,0:T(8,128)} %shard_map.123), calls=%async_computation.1 | async-start | bytes 131072 | tf_op jit(solution)/shard_map/all_to_all | solution.py:335
  46.0 16.9 %all-to-all-start.2 = ((f32[64,1,384]{2,1,0:T(1,128)}), f32[64,1,384]{2,1,0:T(1,128)S(1)}, u32[]{:S(2)}, u32[]{:S(2)}) async-start(f32[64,1,384]{2,1,0:T(1,128)} %shard_map.124), calls=%async_computation.2 | async-start | bytes 196608 | tf_op jit(solution)/shard_map/all_to_all | solution.py:323

commit v7 on v5

--- a/solution.py
+++ b/solution.py
@@ -59,14 +59,16 @@
 def to_rows(pen_ref, cut_ref, dir_in, out_ref, amp_ref, high_ref, low_ref, dir_ref, sem):
     dir_copy = pltpu.make_async_copy(dir_in, dir_ref, sem)
     dir_copy.start()
-    w = lax.broadcasted_iota(i32, (1, KA), 1)
+    w = lax.broadcasted_iota(i32, (1, 128), 1)
     s = lax.broadcasted_iota(i32, (N_SP, 1), 0)
     phase_c, phase_s = turns_to_cos_sin(((s * w) & (N_SP - 1)).astype(f32) * (1.0 / N_SP))
+    phase_c = jnp.concatenate([phase_c, phase_c], axis=1)
+    phase_s = jnp.concatenate([phase_s, phase_s], axis=1)
     r = lax.broadcasted_iota(i32, (ROWS, 1), 0)
-    slot = lax.broadcasted_iota(i32, (1, 2 * KA), 1)
-    ws = jnp.where(slot < KA, slot, jnp.where(slot == KA, KA, slot - KA))
+    w = lax.broadcasted_iota(i32, (1, KA), 1)
+    ws = jnp.where(w == 0, KA, w)
     cos_r, sin_r = turns_to_cos_sin(residue_turns(ws.astype(f32), r.astype(f32), NA))
-    table_high, table_low = split(jnp.where(slot < KA, cos_r, sin_r))
+    table_high, table_low = split(jnp.concatenate([jnp.where(w == 0, 1.0, cos_r), sin_r], axis=1))
     cutoff, pencil = cut_ref[0], pen_ref[0]
     wa = lax.broadcasted_iota(i32, (1, 384), 1)
     wb = lax.broadcasted_iota(i32, (136, 1), 0)
@@ -82,21 +84,24 @@
     amp_ref[...] = amp
 
     dir_copy.wait()
+    nt = ((1,), (1,))
+    pieces = [None] * (LOCAL_M * LOCAL_KB)
     for m in range(LOCAL_M):
         spectral = amp * dir_ref[m]
         part_c = spectral[:, :KA]
         part_s = pltpu.roll(spectral[:, KA:], 1, 1)
         for k in range(LOCAL_KB):
             c, s = part_c[k:k + 1], part_s[k:k + 1]
-            at = pl.ds((k * LOCAL_M + m) * N_SP, N_SP)
+            at = pl.ds((m * LOCAL_KB + k) * N_SP, N_SP)
             for half, value in ((0, c * phase_c + s * phase_s), (1, s * phase_c - c * phase_s)):
                 high, low = split(value)
                 high_ref[at, half * KA:(half + 1) * KA] = high
                 low_ref[at, half * KA:(half + 1) * KA] = low
-    nt = ((1,), (1,))
-    result = (dot(high_ref[...], table_high, nt) + dot(high_ref[...], table_low, nt)
-              + dot(low_ref[...], table_high, nt))
-    pieces = [result[i * N_SP:(i + 1) * N_SP] for i in range(LOCAL_M * LOCAL_KB)]
+        of_m = pl.ds(m * LOCAL_KB * N_SP, LOCAL_KB * N_SP)
+        result = (dot(high_ref[of_m], table_high, nt) + dot(high_ref[of_m], table_low, nt)
+                  + dot(low_ref[of_m], table_high, nt))
+        for k in range(LOCAL_KB):
+            pieces[k * LOCAL_M + m] = result[k * N_SP:(k + 1) * N_SP]
     out_ref[:, 0, :] = jnp.concatenate(pieces, axis=1)
 
 
@@ -206,11 +211,14 @@
 def from_rows(recv_ref, phase_ref, rows_ref, amp_ref, dir_ref, grad_ref, prod_ref, sums_ref):
     count = LOCAL_M * LOCAL_KB
     recv = recv_ref[:, 0, :]
-    left = jnp.concatenate([recv[:, i * ROWS:(i + 1) * ROWS] for i in range(count)], axis=0)
-    high, low = split(left)
-    nn = ((1,), (0,))
+    high, low = split(recv)
+    left = []
+    for i in range(count):
+        at = slice(i * ROWS, (i + 1) * ROWS)
+        left.append(jnp.concatenate([high[:, at], low[:, at], high[:, at]], axis=1))
     table_high, table_low = split(rows_ref[...])
-    turned = dot(high, table_high, nn) + dot(high, table_low, nn) + dot(low, table_high, nn)
+    table = jnp.concatenate([table_high, table_high, table_low], axis=0)
+    turned = dot(jnp.concatenate(left, axis=0), table, ((1,), (0,)))
     phase_c, phase_s = phase_ref[0], phase_ref[1]
     amp = amp_ref[...]
     totals = [jnp.zeros((1, 128), f32)] * 4

time: 88.3 us -> 88.3 us (level)
  no operation moved by 1% of the time
where the time goes in v7:
time: 88.3 us; the launch traced here: 87.8 us
  blocking collectives  40.9 us (46%)
  starting transfers between devices  23.5 us (27%)
  waiting for transfers between devices  9.97 us (11%)
  Pallas kernels  8.96 us (10%)
  local copies, waits for them, and re-layouts  2.44 us (3%)
  between operations  2.04 us (2%)
    all_to_all x2, blocking collectives, share(): return lax.all_to_all(x, axis, 0, 0, axis_index_groups=groups, tiled=True)  24.1 us
    all_to_all x1, starting transfers between devices, swap(): return lax.all_to_all(x, 'sp', 0, 0, tiled=True)  17.1 us
    all_to_all x1, blocking collectives, swap(): return lax.all_to_all(x, 'sp', 0, 0, tiled=True)  16.7 us
    all_to_all x1, starting transfers between devices, share(): return lax.all_to_all(x, axis, 0, 0, axis_index_groups=groups, tiled=True)  6.32 us
    all_to_all x1, waiting for transfers between devices, swap(): return lax.all_to_all(x, 'sp', 0, 0, tiled=True)  5.77 us
    all_to_all x1, waiting for transfers between devices, share(): return lax.all_to_all(x, axis, 0, 0, axis_index_groups=groups, tiled=True)  4.2 us
    pallas_call x1, Pallas kernels, stage_at_slots(): call(at_slots, [VMEM] * 2, [((2, 2 * KB, SLOTS), bf16), ((LOCAL_M, SLOTS)...  3.83 us
    pallas_call x1, Pallas kernels, stage_to_rows(): call(to_rows, [SMEM, SMEM, HBM], [((N_SP, 1, CHUNK), f32), ((LOCAL_KB, 2...  2.07 us
  transfers between devices with their start and end apart: 2, of which 2 were waited for; matrix products, arithmetic and copies ran while one was open for 0% of the time, Pallas kernels for 4%

profile of v7, /device:TPU:1, one launch (start us, length us, event | category | flops | bytes accessed | tf_op | source)
XLA Modules:
  0.0 87.8 jit_solution(3818316459430897852)
XLA Ops:
  1.3 2.1 %shard_map.121 = (f32[64,1,384]{2,1,0:T(1,128)}, f32[4,512]{1,0:T(4,128)}) custom-call(s32[1]{0:T(128)} %bitcast.pen_ref, s32[1]{0:T(128)S(6)} %copy.15.cut_ref, f32[2,4,512]{2,1,0:T(4,128)} %dir_ref.3), custom_call_target="tpu_custom_call" | custom-call | flops 100000000 | bytes 1000000 | tf_op jit(solution)/shard_map/pallas_call | solution.py:278
  3.4 17.1 %all-to-all-start = ((f32[64,1,384]{2,1,0:T(1,128)}), f32[64,1,384]{2,1,0:T(1,128)S(1)}, u32[]{:S(2)}, u32[]{:S(2)}) async-start(f32[64,1,384]{2,1,0:T(1,128)} %get-tuple-element.9), calls=%async_computation | async-start | bytes 196608 | tf_op jit(solution)/shard_map/all_to_all | solution.py:327
  20.5 0.0 copy-start
  20.5 0.7 copy-done
  21.2 0.0 copy-start.6
  21.2 1.1 %copy-done.6 = bf16[2,2,48,1536]{3,2,1,0:T(8,128)(2,1)S(1)} copy-done((bf16[2,2,48,1536]{3,2,1,0:T(8,128)(2,1)S(1)}, bf16[2,2,48,1536]{3,2,1,0:T(8,128)(2,1)}, u32[]{:S(2)}) %copy-start.6) | copy-done | bytes 589848
  22.3 0.0 copy-start.1
  22.3 3.8 %shard_map.122 = (bf16[2,256,2048]{2,1,0:T(8,128)(2,1)S(1)}, f32[2,2048]{1,0:T(2,128)S(1)}) custom-call(s32[1,2048]{1,0:T(1,128)S(1)} %copy-done, bf16[192,1536]{1,0:T(8,128)(2,1)S(1)} %bitcast.5), custom_call_target="tpu_custom_call" | custom-call | flops 2000000000 | bytes 4000000 | tf_op jit(solution)/shard_map/pallas_call | solution.py:288
  26.1 0.0 copy-start.5
  26.1 5.8 %all-to-all-done.recv_ref = f32[64,1,384]{2,1,0:T(1,128)S(1)} async-done(((f32[64,1,384]{2,1,0:T(1,128)}), f32[64,1,384]{2,1,0:T(1,128)S(1)}, u32[]{:S(2)}, u32[]{:S(2)}) %all-to-all-start) | async-done | bytes 98336 | tf_op jit(solution)/shard_map/all_to_all | solution.py:327
  31.9 0.0 copy-done.1
  31.9 0.0 copy-start.2
  31.9 0.0 copy-start.3
  31.9 0.0 copy-start.7
  31.9 0.0 copy-start.8
  31.9 0.0 copy-start.9
  31.9 0.7 shard_map.123
  32.6 0.0 copy-start.4
  32.6 0.6 broadcast_in_dim.8
  33.3 6.3 %all-to-all-start.1 = ((f32[8,16,128]{2,1,0:T(8,128)}), f32[8,16,128]{2,1,0:T(8,128)S(1)}, u32[]{:S(2)}, u32[]{:S(2)}) async-start(f32[8,16,128]{2,1,0:T(8,128)} %broadcast_in_dim.8), calls=%async_computation.1 | async-start | bytes 131072 | tf_op jit(solution)/shard_map/all_to_all | solution.py:332
  40.2 4.2 %all-to-all-done.1.parts_ref = f32[8,16,128]{2,1,0:T(8,128)S(1)} async-done(((f32[8,16,128]{2,1,0:T(8,128)}), f32[8,16,128]{2,1,0:T(8,128)S(1)}, u32[]{:S(2)}, u32[]{:S(2)}) %all-to-all-start.1) | async-done | bytes 65568 | tf_op jit(solution)/shard_map/all_to_all | solution.py:332
  44.4 0.0 copy-done.5
  44.4 0.8 shard_map.124
  45.3 16.7 %all_to_all.25.recv_ref = f32[64,1,384]{2,1,0:T(1,128)S(1)} all-to-all(f32[64,1,384]{2,1,0:T(1,128)S(1)} %shard_map.124), channel_id=1, replica_groups=mesh['mem'=8,'sp'=64] {'sp'}, dimensions={0} | all-to-all | bytes 196608 | tf_op jit(solution)/shard_map/all_to_all | solution.py:327
  62.0 0.0 copy-done.2
  62.0 0.0 copy-done.3
  62.0 0.0 copy-done.7
  62.0 0.0 copy-done.8
  62.0 0.0 copy-done.9
  62.0 0.8 shard_map.125
  62.9 10.2 %all_to_all.26 = f32[16,1,128]{2,1,0:T(1,128)S(1)} all-to-all(f32[16,1,128]{2,1,0:T(1,128)S(1)} %broadcast_in_dim.10), channel_id=1, replica_groups={{0,1,64,65,128,129,192,193,256,257,320,321,384,385,448,449},{2,3,66,67,..., dimensions={0} | all-to-all | bytes 16384 | tf_op jit(solution)/shard_map/all_to_all | solution.py:332
  73.1 14.0 %all_to_all.27.parts_ref = f32[32,1,128]{2,1,0:T(1,128)S(1)} all-to-all(f32[32,1,128]{2,1,0:T(1,128)S(1)} %broadcast_in_dim.11), channel_id=1, replica_groups={{0,2,4,6,8,10,12,14,16,18,20,22,24,26,28,30,32,34,36,38,40,42,44,46,48,..., dimensions={0} | all-to-all | bytes 32768 | tf_op jit(solution)/shard_map/all_to_all | solution.py:332
  87.0 0.0 copy-done.4
  87.0 0.7 shard_map.126
  (3 shorter events, 0.0 us)
Async XLA Ops:
  3.4 28.5 %all-to-all-start = ((f32[64,1,384]{2,1,0:T(1,128)}), f32[64,1,384]{2,1,0:T(1,128)S(1)}, u32[]{:S(2)}, u32[]{:S(2)}) async-start(f32[64,1,384]{2,1,0:T(1,128)} %get-tuple-element.9), calls=%async_computation | async-start | bytes 196608 | tf_op jit(solution)/shard_map/all_to_all | solution.py:327
  20.5 0.7 copy-start
  21.2 1.1 %copy-start.6 = (bf16[2,2,48,1536]{3,2,1,0:T(8,128)(2,1)S(1)}, bf16[2,2,48,1536]{3,2,1,0:T(8,128)(2,1)}, u32[]{:S(2)}) copy-start(bf16[2,2,48,1536]{3,2,1,0:T(8,128)(2,1)} %param.13) | copy-start | bytes 1769476
  22.3 9.6 %copy-start.1 = (s32[1,2048]{1,0:T(1,128)S(1)}, s32[1,2048]{1,0:T(1,128)}, u32[]{:S(2)}) copy-start(s32[1,2048]{1,0:T(1,128)} %index_ref.5) | copy-start | bytes 24580
  26.1 18.3 %copy-start.5 = (f32[1,2048]{1,0:T(1,128)S(1)}, f32[1,2048]{1,0:T(1,128)}, u32[]{:S(2)}) copy-start(f32[1,2048]{1,0:T(1,128)} %weight_ref.1) | copy-start | bytes 24580
  31.9 30.1 %copy-start.2 = (f32[2,4,512]{2,1,0:T(4,128)S(1)}, f32[2,4,512]{2,1,0:T(4,128)}, u32[]{:S(2)}) copy-start(f32[2,4,512]{2,1,0:T(4,128)} %dir_ref.3) | copy-start | bytes 49156
  31.9 30.1 %copy-start.3 = (f32[2,4,512]{2,1,0:T(4,128)S(1)}, f32[2,4,512]{2,1,0:T(4,128)}, u32[]{:S(2)}) copy-start(f32[2,4,512]{2,1,0:T(4,128)} %grad_ref.3) | copy-start | bytes 49156
  31.9 30.1 %copy-start.7 = (f32[2,64,256]{2,1,0:T(8,128)S(1)}, f32[2,64,256]{2,1,0:T(8,128)}, u32[]{:S(2)}) copy-start(f32[2,64,256]{2,1,0:T(8,128)} %constant.10.clone.phase_ref) | copy-start | bytes 393220
  31.9 30.1 %copy-start.8 = (f32[48,512]{1,0:T(8,128)S(1)}, f32[48,512]{1,0:T(8,128)}, u32[]{:S(2)}) copy-start(f32[48,512]{1,0:T(8,128)} %constant.11.clone.rows_ref) | copy-start | bytes 294916
  31.9 30.1 %copy-start.9 = (f32[4,512]{1,0:T(4,128)S(1)}, f32[4,512]{1,0:T(4,128)}, u32[]{:S(2)}) copy-start(f32[4,512]{1,0:T(4,128)} %get-tuple-element.12.amp_ref) | copy-start | bytes 24580
  32.6 54.4 %copy-start.4 = (f32[2,4,512]{2,1,0:T(4,128)S(1)}, f32[2,4,512]{2,1,0:T(4,128)}, u32[]{:S(2)}) copy-start(f32[2,4,512]{2,1,0:T(4,128)} %cont_ref.1) | copy-start | bytes 49156
  33.3 11.2 %all-to-all-start.1 = ((f32[8,16,128]{2,1,0:T(8,128)}), f32[8,16,128]{2,1,0:T(8,128)S(1)}, u32[]{:S(2)}, u32[]{:S(2)}) async-start(f32[8,16,128]{2,1,0:T(8,128)} %broadcast_in_dim.8), calls=%async_computation.1 | async-start | bytes 131072 | tf_op jit(solution)/shard_map/all_to_all | solution.py:332

commit v8 on v7

--- a/solution.py
+++ b/solution.py
@@ -319,17 +319,13 @@
     )(parts, control, gradient, direction, product)
 
 
-NEAR = [[m * N_SP + s + y for m in range(SIDE) for y in range(2)] for s in range(0, N_SP, 2)]
-FAR = [[m * N_SP + s + y for s in range(0, N_SP, 2)] for m in range(SIDE) for y in range(2)]
-
-
 def swap(x):
     return lax.all_to_all(x, "sp", 0, 0, tiled=True)
 
 
-def share(x, axis, count, groups=None):
+def share(x, axis, count):
     x = jnp.broadcast_to(x[None], (count,) + x.shape)
-    return lax.all_to_all(x, axis, 0, 0, axis_index_groups=groups, tiled=True)
+    return lax.all_to_all(x, axis, 0, 0, tiled=True)
 
 
 def shards(phase, rows, control, gradient, direction, perturb, obs_index, obs_count, obs_weight, cutoff):
@@ -339,8 +335,8 @@
     part = stage_sample(swap(send), basis, values, obs_index)
     send = stage_spread(obs_count, share(part, "mem", SIDE), obs_weight, basis, values, obs_index)
     product, sums = stage_from_rows(swap(send), phase, rows, amp, direction, gradient)
-    sums = jnp.sum(share(sums, ("mem", "sp"), len(NEAR[0]), NEAR), axis=0)
-    sums = share(sums, ("mem", "sp"), len(FAR[0]), FAR)
+    sums = jnp.sum(share(sums, "mem", SIDE), axis=0)
+    sums = share(sums, "sp", N_SP)
     return tuple(stage_update(sums, control, gradient, direction, product))
 
 

time: 88.3 us -> 88 us (level)
  no operation moved by 1% of the time
where the time goes in v8:
time: 88 us; the launch traced here: 87.5 us
  blocking collectives  40.5 us (46%)
  starting transfers between devices  23.5 us (27%)
  waiting for transfers between devices  9.97 us (11%)
  Pallas kernels  9 us (10%)
  local copies, waits for them, and re-layouts  2.45 us (3%)
  between operations  2.05 us (2%)
    all_to_all x2, blocking collectives, share(): return lax.all_to_all(x, axis, 0, 0, tiled=True)  23.8 us
    all_to_all x1, starting transfers between devices, swap(): return lax.all_to_all(x, 'sp', 0, 0, tiled=True)  17.1 us
    all_to_all x1, blocking collectives, swap(): return lax.all_to_all(x, 'sp', 0, 0, tiled=True)  16.7 us
    all_to_all x1, starting transfers between devices, share(): return lax.all_to_all(x, axis, 0, 0, tiled=True)  6.32 us
    all_to_all x1, waiting for transfers between devices, swap(): return lax.all_to_all(x, 'sp', 0, 0, tiled=True)  5.77 us
    all_to_all x1, waiting for transfers between devices, share(): return lax.all_to_all(x, axis, 0, 0, tiled=True)  4.2 us
    pallas_call x1, Pallas kernels, stage_at_slots(): call(at_slots, [VMEM] * 2, [((2, 2 * KB, SLOTS), bf16), ((LOCAL_M, SLOTS)...  3.83 us
    pallas_call x1, Pallas kernels, stage_to_rows(): call(to_rows, [SMEM, SMEM, HBM], [((N_SP, 1, CHUNK), f32), ((LOCAL_KB, 2...  2.07 us
  transfers between devices with their start and end apart: 2, of which 2 were waited for; matrix products, arithmetic and copies ran while one was open for 0% of the time, Pallas kernels for 4%

profile of v8, /device:TPU:1, one launch (start us, length us, event | category | flops | bytes accessed | tf_op | source)
XLA Modules:
  0.0 87.5 jit_solution(14353368833118263934)
XLA Ops:
  1.3 2.1 %shard_map.121 = (f32[64,1,384]{2,1,0:T(1,128)}, f32[4,512]{1,0:T(4,128)}) custom-call(s32[1]{0:T(128)} %bitcast.pen_ref, s32[1]{0:T(128)S(6)} %copy.15.cut_ref, f32[2,4,512]{2,1,0:T(4,128)} %dir_ref.3), custom_call_target="tpu_custom_call" | custom-call | flops 100000000 | bytes 1000000 | tf_op jit(solution)/shard_map/pallas_call | solution.py:278
  3.4 17.1 %all-to-all-start = ((f32[64,1,384]{2,1,0:T(1,128)}), f32[64,1,384]{2,1,0:T(1,128)S(1)}, u32[]{:S(2)}, u32[]{:S(2)}) async-start(f32[64,1,384]{2,1,0:T(1,128)} %get-tuple-element.9), calls=%async_computation | async-start | bytes 196608 | tf_op jit(solution)/shard_map/all_to_all | solution.py:323
  20.5 0.0 copy-start
  20.5 0.7 copy-done
  21.2 0.0 copy-start.6
  21.2 1.1 %copy-done.6 = bf16[2,2,48,1536]{3,2,1,0:T(8,128)(2,1)S(1)} copy-done((bf16[2,2,48,1536]{3,2,1,0:T(8,128)(2,1)S(1)}, bf16[2,2,48,1536]{3,2,1,0:T(8,128)(2,1)}, u32[]{:S(2)}) %copy-start.6) | copy-done | bytes 589848
  22.3 0.0 copy-start.1
  22.3 3.8 %shard_map.122 = (bf16[2,256,2048]{2,1,0:T(8,128)(2,1)S(1)}, f32[2,2048]{1,0:T(2,128)S(1)}) custom-call(s32[1,2048]{1,0:T(1,128)S(1)} %copy-done, bf16[192,1536]{1,0:T(8,128)(2,1)S(1)} %bitcast.5), custom_call_target="tpu_custom_call" | custom-call | flops 2000000000 | bytes 4000000 | tf_op jit(solution)/shard_map/pallas_call | solution.py:288
  26.1 0.0 copy-start.5
  26.1 5.8 %all-to-all-done.recv_ref = f32[64,1,384]{2,1,0:T(1,128)S(1)} async-done(((f32[64,1,384]{2,1,0:T(1,128)}), f32[64,1,384]{2,1,0:T(1,128)S(1)}, u32[]{:S(2)}, u32[]{:S(2)}) %all-to-all-start) | async-done | bytes 98336 | tf_op jit(solution)/shard_map/all_to_all | solution.py:323
  31.9 0.0 copy-done.1
  31.9 0.0 copy-start.2
  31.9 0.0 copy-start.3
  31.9 0.0 copy-start.7
  31.9 0.0 copy-start.8
  31.9 0.0 copy-start.9
  31.9 0.7 shard_map.123
  32.6 0.0 copy-start.4
  32.6 0.6 broadcast_in_dim.8
  33.3 6.3 %all-to-all-start.1 = ((f32[8,16,128]{2,1,0:T(8,128)}), f32[8,16,128]{2,1,0:T(8,128)S(1)}, u32[]{:S(2)}, u32[]{:S(2)}) async-start(f32[8,16,128]{2,1,0:T(8,128)} %broadcast_in_dim.8), calls=%async_computation.1 | async-start | bytes 131072 | tf_op jit(solution)/shard_map/all_to_all | solution.py:328
  40.2 4.2 %all-to-all-done.1.parts_ref = f32[8,16,128]{2,1,0:T(8,128)S(1)} async-done(((f32[8,16,128]{2,1,0:T(8,128)}), f32[8,16,128]{2,1,0:T(8,128)S(1)}, u32[]{:S(2)}, u32[]{:S(2)}) %all-to-all-start.1) | async-done | bytes 65568 | tf_op jit(solution)/shard_map/all_to_all | solution.py:328
  44.4 0.0 copy-done.5
  44.4 0.8 shard_map.124
  45.3 16.7 %all_to_all.25.recv_ref = f32[64,1,384]{2,1,0:T(1,128)S(1)} all-to-all(f32[64,1,384]{2,1,0:T(1,128)S(1)} %shard_map.124), channel_id=1, replica_groups=mesh['mem'=8,'sp'=64] {'sp'}, dimensions={0} | all-to-all | bytes 196608 | tf_op jit(solution)/shard_map/all_to_all | solution.py:323
  62.0 0.0 copy-done.2
  62.0 0.0 copy-done.3
  62.0 0.0 copy-done.7
  62.0 0.0 copy-done.8
  62.0 0.0 copy-done.9
  62.0 0.8 shard_map.125
  62.9 9.1 %all_to_all.26 = f32[8,1,128]{2,1,0:T(1,128)S(1)} all-to-all(f32[8,1,128]{2,1,0:T(1,128)S(1)} %broadcast_in_dim.10), channel_id=1, replica_groups=mesh['mem'=8,'sp'=64] {'mem'}, dimensions={0} | all-to-all | bytes 8192 | tf_op jit(solution)/shard_map/all_to_all | solution.py:328
  72.0 14.6 %all_to_all.27.parts_ref = f32[64,1,128]{2,1,0:T(1,128)S(1)} all-to-all(f32[64,1,128]{2,1,0:T(1,128)S(1)} %broadcast_in_dim.11), channel_id=1, replica_groups=mesh['mem'=8,'sp'=64] {'sp'}, dimensions={0} | all-to-all | bytes 65536 | tf_op jit(solution)/shard_map/all_to_all | solution.py:328
  86.7 0.0 copy-done.4
  86.7 0.8 shard_map.126
  (3 shorter events, 0.0 us)
Async XLA Ops:
  3.4 28.5 %all-to-all-start = ((f32[64,1,384]{2,1,0:T(1,128)}), f32[64,1,384]{2,1,0:T(1,128)S(1)}, u32[]{:S(2)}, u32[]{:S(2)}) async-start(f32[64,1,384]{2,1,0:T(1,128)} %get-tuple-element.9), calls=%async_computation | async-start | bytes 196608 | tf_op jit(solution)/shard_map/all_to_all | solution.py:323
  20.5 0.7 copy-start
  21.2 1.1 %copy-start.6 = (bf16[2,2,48,1536]{3,2,1,0:T(8,128)(2,1)S(1)}, bf16[2,2,48,1536]{3,2,1,0:T(8,128)(2,1)}, u32[]{:S(2)}) copy-start(bf16[2,2,48,1536]{3,2,1,0:T(8,128)(2,1)} %param.13) | copy-start | bytes 1769476
  22.3 9.6 %copy-start.1 = (s32[1,2048]{1,0:T(1,128)S(1)}, s32[1,2048]{1,0:T(1,128)}, u32[]{:S(2)}) copy-start(s32[1,2048]{1,0:T(1,128)} %index_ref.5) | copy-start | bytes 24580
  26.1 18.3 %copy-start.5 = (f32[1,2048]{1,0:T(1,128)S(1)}, f32[1,2048]{1,0:T(1,128)}, u32[]{:S(2)}) copy-start(f32[1,2048]{1,0:T(1,128)} %weight_ref.1) | copy-start | bytes 24580
  31.9 30.1 %copy-start.2 = (f32[2,4,512]{2,1,0:T(4,128)S(1)}, f32[2,4,512]{2,1,0:T(4,128)}, u32[]{:S(2)}) copy-start(f32[2,4,512]{2,1,0:T(4,128)} %dir_ref.3) | copy-start | bytes 49156
  31.9 30.1 %copy-start.3 = (f32[2,4,512]{2,1,0:T(4,128)S(1)}, f32[2,4,512]{2,1,0:T(4,128)}, u32[]{:S(2)}) copy-start(f32[2,4,512]{2,1,0:T(4,128)} %grad_ref.3) | copy-start | bytes 49156
  31.9 30.1 %copy-start.7 = (f32[2,64,256]{2,1,0:T(8,128)S(1)}, f32[2,64,256]{2,1,0:T(8,128)}, u32[]{:S(2)}) copy-start(f32[2,64,256]{2,1,0:T(8,128)} %constant.10.clone.phase_ref) | copy-start | bytes 393220
  31.9 30.1 %copy-start.8 = (f32[48,512]{1,0:T(8,128)S(1)}, f32[48,512]{1,0:T(8,128)}, u32[]{:S(2)}) copy-start(f32[48,512]{1,0:T(8,128)} %constant.11.clone.rows_ref) | copy-start | bytes 294916
  31.9 30.1 %copy-start.9 = (f32[4,512]{1,0:T(4,128)S(1)}, f32[4,512]{1,0:T(4,128)}, u32[]{:S(2)}) copy-start(f32[4,512]{1,0:T(4,128)} %get-tuple-element.12.amp_ref) | copy-start | bytes 24580
  32.6 54.1 %copy-start.4 = (f32[2,4,512]{2,1,0:T(4,128)S(1)}, f32[2,4,512]{2,1,0:T(4,128)}, u32[]{:S(2)}) copy-start(f32[2,4,512]{2,1,0:T(4,128)} %cont_ref.1) | copy-start | bytes 49156
  33.3 11.2 %all-to-all-start.1 = ((f32[8,16,128]{2,1,0:T(8,128)}), f32[8,16,128]{2,1,0:T(8,128)S(1)}, u32[]{:S(2)}, u32[]{:S(2)}) async-start(f32[8,16,128]{2,1,0:T(8,128)} %broadcast_in_dim.8), calls=%async_computation.1 | async-start | bytes 131072 | tf_op jit(solution)/shard_map/all_to_all | solution.py:328

commit v9 on v8

--- a/solution.py
+++ b/solution.py
@@ -69,6 +69,8 @@
     ws = jnp.where(w == 0, KA, w)
     cos_r, sin_r = turns_to_cos_sin(residue_turns(ws.astype(f32), r.astype(f32), NA))
     table_high, table_low = split(jnp.concatenate([jnp.where(w == 0, 1.0, cos_r), sin_r], axis=1))
+    empty = jnp.zeros((128 - ROWS, 2 * KA), bf16)
+    table_both = jnp.concatenate([table_high, empty, table_low, empty], axis=0)
     cutoff, pencil = cut_ref[0], pen_ref[0]
     wa = lax.broadcasted_iota(i32, (1, 384), 1)
     wb = lax.broadcasted_iota(i32, (136, 1), 0)
@@ -98,8 +100,8 @@
                 high_ref[at, half * KA:(half + 1) * KA] = high
                 low_ref[at, half * KA:(half + 1) * KA] = low
         of_m = pl.ds(m * LOCAL_KB * N_SP, LOCAL_KB * N_SP)
-        result = (dot(high_ref[of_m], table_high, nt) + dot(high_ref[of_m], table_low, nt)
-                  + dot(low_ref[of_m], table_high, nt))
+        both = dot(high_ref[of_m], table_both, nt)
+        result = both[:, :ROWS] + both[:, 128:128 + ROWS] + dot(low_ref[of_m], table_high, nt)
         for k in range(LOCAL_KB):
             pieces[k * LOCAL_M + m] = result[k * N_SP:(k + 1) * N_SP]
     out_ref[:, 0, :] = jnp.concatenate(pieces, axis=1)

time: 88 us -> 87.9 us (level)
  no operation moved by 1% of the time
where the time goes in v9:
time: 87.9 us; the launch traced here: 87.3 us
  blocking collectives  40.5 us (46%)
  starting transfers between devices  23.5 us (27%)
  waiting for transfers between devices  9.97 us (11%)
  Pallas kernels  8.88 us (10%)
  local copies, waits for them, and re-layouts  2.45 us (3%)
  between operations  2.05 us (2%)
    all_to_all x2, blocking collectives, share(): return lax.all_to_all(x, axis, 0, 0, tiled=True)  23.8 us
    all_to_all x1, starting transfers between devices, swap(): return lax.all_to_all(x, 'sp', 0, 0, tiled=True)  17.1 us
    all_to_all x1, blocking collectives, swap(): return lax.all_to_all(x, 'sp', 0, 0, tiled=True)  16.7 us
    all_to_all x1, starting transfers between devices, share(): return lax.all_to_all(x, axis, 0, 0, tiled=True)  6.32 us
    all_to_all x1, waiting for transfers between devices, swap(): return lax.all_to_all(x, 'sp', 0, 0, tiled=True)  5.77 us
    all_to_all x1, waiting for transfers between devices, share(): return lax.all_to_all(x, axis, 0, 0, tiled=True)  4.2 us
    pallas_call x1, Pallas kernels, stage_at_slots(): call(at_slots, [VMEM] * 2, [((2, 2 * KB, SLOTS), bf16), ((LOCAL_M, SLOTS)...  3.83 us
    pallas_call x1, Pallas kernels, stage_to_rows(): call(to_rows, [SMEM, SMEM, HBM], [((N_SP, 1, CHUNK), f32), ((LOCAL_KB, 2...  1.95 us
  transfers between devices with their start and end apart: 2, of which 2 were waited for; matrix products, arithmetic and copies ran while one was open for 0% of the time, Pallas kernels for 4%

profile of v9, /device:TPU:1, one launch (start us, length us, event | category | flops | bytes accessed | tf_op | source)
XLA Modules:
  0.0 87.3 jit_solution(17377127243411848085)
XLA Ops:
  1.3 2.0 %shard_map.121 = (f32[64,1,384]{2,1,0:T(1,128)}, f32[4,512]{1,0:T(4,128)}) custom-call(s32[1]{0:T(128)} %bitcast.pen_ref, s32[1]{0:T(128)S(6)} %copy.15.cut_ref, f32[2,4,512]{2,1,0:T(4,128)} %dir_ref.3), custom_call_target="tpu_custom_call" | custom-call | flops 100000000 | bytes 1000000 | tf_op jit(solution)/shard_map/pallas_call | solution.py:280
  3.2 17.1 %all-to-all-start = ((f32[64,1,384]{2,1,0:T(1,128)}), f32[64,1,384]{2,1,0:T(1,128)S(1)}, u32[]{:S(2)}, u32[]{:S(2)}) async-start(f32[64,1,384]{2,1,0:T(1,128)} %get-tuple-element.9), calls=%async_computation | async-start | bytes 196608 | tf_op jit(solution)/shard_map/all_to_all | solution.py:325
  20.4 0.0 copy-start
  20.4 0.7 copy-done
  21.1 0.0 copy-start.6
  21.1 1.1 %copy-done.6 = bf16[2,2,48,1536]{3,2,1,0:T(8,128)(2,1)S(1)} copy-done((bf16[2,2,48,1536]{3,2,1,0:T(8,128)(2,1)S(1)}, bf16[2,2,48,1536]{3,2,1,0:T(8,128)(2,1)}, u32[]{:S(2)}) %copy-start.6) | copy-done | bytes 589848
  22.2 0.0 copy-start.1
  22.2 3.8 %shard_map.122 = (bf16[2,256,2048]{2,1,0:T(8,128)(2,1)S(1)}, f32[2,2048]{1,0:T(2,128)S(1)}) custom-call(s32[1,2048]{1,0:T(1,128)S(1)} %copy-done, bf16[192,1536]{1,0:T(8,128)(2,1)S(1)} %bitcast.5), custom_call_target="tpu_custom_call" | custom-call | flops 2000000000 | bytes 4000000 | tf_op jit(solution)/shard_map/pallas_call | solution.py:290
  26.0 0.0 copy-start.5
  26.0 5.8 %all-to-all-done.recv_ref = f32[64,1,384]{2,1,0:T(1,128)S(1)} async-done(((f32[64,1,384]{2,1,0:T(1,128)}), f32[64,1,384]{2,1,0:T(1,128)S(1)}, u32[]{:S(2)}, u32[]{:S(2)}) %all-to-all-start) | async-done | bytes 98336 | tf_op jit(solution)/shard_map/all_to_all | solution.py:325
  31.8 0.0 copy-done.1
  31.8 0.0 copy-start.2
  31.8 0.0 copy-start.3
  31.8 0.0 copy-start.7
  31.8 0.0 copy-start.8
  31.8 0.0 copy-start.9
  31.8 0.7 shard_map.123
  32.5 0.0 copy-start.4
  32.5 0.6 broadcast_in_dim.8
  33.1 6.3 %all-to-all-start.1 = ((f32[8,16,128]{2,1,0:T(8,128)}), f32[8,16,128]{2,1,0:T(8,128)S(1)}, u32[]{:S(2)}, u32[]{:S(2)}) async-start(f32[8,16,128]{2,1,0:T(8,128)} %broadcast_in_dim.8), calls=%async_computation.1 | async-start | bytes 131072 | tf_op jit(solution)/shard_map/all_to_all | solution.py:330
  40.1 4.2 %all-to-all-done.1.parts_ref = f32[8,16,128]{2,1,0:T(8,128)S(1)} async-done(((f32[8,16,128]{2,1,0:T(8,128)}), f32[8,16,128]{2,1,0:T(8,128)S(1)}, u32[]{:S(2)}, u32[]{:S(2)}) %all-to-all-start.1) | async-done | bytes 65568 | tf_op jit(solution)/shard_map/all_to_all | solution.py:330
  44.3 0.0 copy-done.5
  44.3 0.8 shard_map.124
  45.2 16.7 %all_to_all.25.recv_ref = f32[64,1,384]{2,1,0:T(1,128)S(1)} all-to-all(f32[64,1,384]{2,1,0:T(1,128)S(1)} %shard_map.124), channel_id=1, replica_groups=mesh['mem'=8,'sp'=64] {'sp'}, dimensions={0} | all-to-all | bytes 196608 | tf_op jit(solution)/shard_map/all_to_all | solution.py:325
  61.9 0.0 copy-done.2
  61.9 0.0 copy-done.3
  61.9 0.0 copy-done.7
  61.9 0.0 copy-done.8
  61.9 0.0 copy-done.9
  61.9 0.8 shard_map.125
  62.7 9.1 %all_to_all.26 = f32[8,1,128]{2,1,0:T(1,128)S(1)} all-to-all(f32[8,1,128]{2,1,0:T(1,128)S(1)} %broadcast_in_dim.10), channel_id=1, replica_groups=mesh['mem'=8,'sp'=64] {'mem'}, dimensions={0} | all-to-all | bytes 8192 | tf_op jit(solution)/shard_map/all_to_all | solution.py:330
  71.9 14.6 %all_to_all.27.parts_ref = f32[64,1,128]{2,1,0:T(1,128)S(1)} all-to-all(f32[64,1,128]{2,1,0:T(1,128)S(1)} %broadcast_in_dim.11), channel_id=1, replica_groups=mesh['mem'=8,'sp'=64] {'sp'}, dimensions={0} | all-to-all | bytes 65536 | tf_op jit(solution)/shard_map/all_to_all | solution.py:330
  86.6 0.0 copy-done.4
  86.6 0.8 shard_map.126
  (3 shorter events, 0.0 us)
Async XLA Ops:
  3.2 28.5 %all-to-all-start = ((f32[64,1,384]{2,1,0:T(1,128)}), f32[64,1,384]{2,1,0:T(1,128)S(1)}, u32[]{:S(2)}, u32[]{:S(2)}) async-start(f32[64,1,384]{2,1,0:T(1,128)} %get-tuple-element.9), calls=%async_computation | async-start | bytes 196608 | tf_op jit(solution)/shard_map/all_to_all | solution.py:325
  20.4 0.7 copy-start
  21.1 1.1 %copy-start.6 = (bf16[2,2,48,1536]{3,2,1,0:T(8,128)(2,1)S(1)}, bf16[2,2,48,1536]{3,2,1,0:T(8,128)(2,1)}, u32[]{:S(2)}) copy-start(bf16[2,2,48,1536]{3,2,1,0:T(8,128)(2,1)} %param.13) | copy-start | bytes 1769476
  22.2 9.6 %copy-start.1 = (s32[1,2048]{1,0:T(1,128)S(1)}, s32[1,2048]{1,0:T(1,128)}, u32[]{:S(2)}) copy-start(s32[1,2048]{1,0:T(1,128)} %index_ref.5) | copy-start | bytes 24580
  26.0 18.3 %copy-start.5 = (f32[1,2048]{1,0:T(1,128)S(1)}, f32[1,2048]{1,0:T(1,128)}, u32[]{:S(2)}) copy-start(f32[1,2048]{1,0:T(1,128)} %weight_ref.1) | copy-start | bytes 24580
  31.8 30.1 %copy-start.2 = (f32[2,4,512]{2,1,0:T(4,128)S(1)}, f32[2,4,512]{2,1,0:T(4,128)}, u32[]{:S(2)}) copy-start(f32[2,4,512]{2,1,0:T(4,128)} %dir_ref.3) | copy-start | bytes 49156
  31.8 30.1 %copy-start.3 = (f32[2,4,512]{2,1,0:T(4,128)S(1)}, f32[2,4,512]{2,1,0:T(4,128)}, u32[]{:S(2)}) copy-start(f32[2,4,512]{2,1,0:T(4,128)} %grad_ref.3) | copy-start | bytes 49156
  31.8 30.1 %copy-start.7 = (f32[2,64,256]{2,1,0:T(8,128)S(1)}, f32[2,64,256]{2,1,0:T(8,128)}, u32[]{:S(2)}) copy-start(f32[2,64,256]{2,1,0:T(8,128)} %constant.10.clone.phase_ref) | copy-start | bytes 393220
  31.8 30.1 %copy-start.8 = (f32[48,512]{1,0:T(8,128)S(1)}, f32[48,512]{1,0:T(8,128)}, u32[]{:S(2)}) copy-start(f32[48,512]{1,0:T(8,128)} %constant.11.clone.rows_ref) | copy-start | bytes 294916
  31.8 30.1 %copy-start.9 = (f32[4,512]{1,0:T(4,128)S(1)}, f32[4,512]{1,0:T(4,128)}, u32[]{:S(2)}) copy-start(f32[4,512]{1,0:T(4,128)} %get-tuple-element.12.amp_ref) | copy-start | bytes 24580
  32.5 54.1 %copy-start.4 = (f32[2,4,512]{2,1,0:T(4,128)S(1)}, f32[2,4,512]{2,1,0:T(4,128)}, u32[]{:S(2)}) copy-start(f32[2,4,512]{2,1,0:T(4,128)} %cont_ref.1) | copy-start | bytes 49156
  33.1 11.2 %all-to-all-start.1 = ((f32[8,16,128]{2,1,0:T(8,128)}), f32[8,16,128]{2,1,0:T(8,128)S(1)}, u32[]{:S(2)}, u32[]{:S(2)}) async-start(f32[8,16,128]{2,1,0:T(8,128)} %broadcast_in_dim.8), calls=%async_computation.1 | async-start | bytes 131072 | tf_op jit(solution)/shard_map/all_to_all | solution.py:330
